TPU v7x, 128 devices: a whole 4x4x4 slice. The times are simulated.
128 devices in a mesh: row: 8 (over y, x_hi), col: 16 (over z, x_lo, core).
Axes of the slice: x: 4 (x_hi: 2, x_lo: 2; x = x_hi * 2 + x_lo), y: 4, z: 4, core: 2. Of those that a mesh axis runs over, the one named last changes fastest.
Arguments:
- polarization: bfloat16 [4096, 26624], P('row', 'col'), may hold values from -6 to 6
- metric: bfloat16 [26624, 4096], P('row', 'col'), may hold values from -0.0390625 to 0.0390625
- three_panel: bfloat16 [4096, 64, 256], P('row'), may hold values from -0.125 to 0.125
- three_near: bfloat16 [4096, 64, 256], P('col'), may hold values from -0.0078125 to 0.0078125
- green_function: bfloat16 [256, 256], replicated, may hold values from -0.375 to 0.375
- mask_panel: int32 [64, 8], replicated, may hold values 0 or 1
- mask_near: int32 [64, 8], replicated, may hold values 0 or 1
Outputs:
- screened: bfloat16 [4096, 4096], P('row', 'col')
- contracted: bfloat16 [4096, 64, 256], P('col', None, 'row')
- self_energy: float32 [64, 64], P('row', 'col')
All inputs are finite; a program needn't handle non-finite values.
Results may differ from a plain program's by a relative error of at most 0.02.
Values may be sent and summed in bfloat16 or wider, within the bound.
A program may use at most 192 MiB of HBM per device.

v0:
```python
import jax
import jax.numpy as jnp
from jax import lax
from jax.sharding import PartitionSpec as P

TILE = 64
NL = 256
RB = 64
AB = 32


def expand_mask(mask, rows, cols):
    return jnp.repeat(jnp.repeat(mask, rows, axis=0), cols, axis=1)


def per_device(
    polarization, metric, three_panel, three_near, green_function, mask_panel, mask_near
):
    row_index = lax.axis_index("row")
    col_index = lax.axis_index("col")
    row_count = lax.axis_size("row")
    panel_rows = polarization.shape[0]
    near_cols = metric.shape[1]
    metric_full = lax.all_gather(metric, "row", axis=0, tiled=True)
    screened_sum = jnp.dot(
        lax.all_gather(polarization, "col", axis=1, tiled=True),
        metric_full,
        preferred_element_type=jnp.float32,
    )
    screened = screened_sum.astype(jnp.bfloat16)
    panel_blocks = panel_rows // RB
    panel_mask = lax.dynamic_slice_in_dim(mask_panel, row_index * panel_blocks, panel_blocks, 0)
    panel = three_panel * expand_mask(panel_mask, RB, AB).astype(jnp.bfloat16)[:, None, :]
    near_blocks = near_cols // RB
    near_mask = lax.dynamic_slice_in_dim(mask_near, col_index * near_blocks, near_blocks, 0)
    near = three_near * expand_mask(near_mask, RB, AB).astype(jnp.bfloat16)[:, None, :]
    near_flat = near.reshape(near_cols * TILE, NL)
    contract_part = lax.dot_general(
        screened,
        panel.reshape(panel_rows, TILE * NL),
        (((0,), (0,)), ((), ())),
        preferred_element_type=jnp.float32,
    )
    contract_part = (
        contract_part.astype(jnp.bfloat16).astype(jnp.float32).reshape(near_cols, TILE, NL)
    )
    near_share = NL // row_count
    contracted = lax.psum(contract_part.astype(jnp.bfloat16), "row")
    dressed = jnp.dot(near_flat, green_function.T, preferred_element_type=jnp.float32)
    dressed = dressed.astype(jnp.bfloat16).reshape(near_cols, TILE, NL)
    tile_part = -lax.dot_general(
        contracted, dressed, (((0, 2), (0, 2)), ((), ())), preferred_element_type=jnp.float32
    )
    column_share = lax.psum_scatter(tile_part, "col", scatter_dimension=1, tiled=True)
    row_share = TILE // row_count
    self_energy = lax.dynamic_slice_in_dim(column_share, row_index * row_share, row_share, 0)
    contracted_out = lax.dynamic_slice_in_dim(contracted, row_index * near_share, near_share, 2)
    return (screened, contracted_out, self_energy)


def solution(mesh):
    placed = (
        P("row", "col"),
        P("row", "col"),
        P("row", None, None),
        P("col", None, None),
        P(),
        P(),
        P(),
    )
    return jax.shard_map(
        per_device,
        mesh=mesh,
        in_specs=placed,
        out_specs=(P("row", "col"), P("col", None, "row"), P("row", "col")),
        check_vma=False,
    )
```

profile of v0, /device:TPU:1, one launch (start us, length us, event | category | flops | bytes accessed | tf_op | source)
XLA Modules:
  0.0 767.5 jit_solution(14037136357439026897)
XLA Ops:
  7.2 0.0 copy-start
  7.2 0.0 all-gather.5.cloned.1.call-start
  7.2 0.7 all-gather.5.cloned.1.call-update
  7.9 0.0 all-gather.3.cloned.1.call-start
  8.0 0.7 all-gather.3.cloned.1.call-update
  8.7 0.0 all-reduce.3.cloned.1.call-start
  8.7 0.8 dynamic-slice_convert_fusion.1
  9.5 0.1 broadcast_in_dim.14
  9.6 0.1 convert_element_type.46
  9.7 0.1 copy.16
  9.8 8.0 %broadcast_multiply_fusion = bf16[512,64,256]{2,1,0:T(8,128)(2,1)S(1)} fusion(bf16[512,64,256]{2,1,0:T(8,128)(2,1)} %param.9, bf16[512,256]{1,0:T(8,128)(2,1)S(1)} %copy.16), kind=kLoop, calls=%fused_computation.2 | loop fusion | flops 8388608 | bytes 33816576 | tf_op jit(solution)/shard_map/mul | solution.py:33
  17.9 12.5 %copy.19 = bf16[64,8,64,256]{3,1,2,0:T(8,128)(2,1)} copy(bf16[64,8,64,256]{3,2,1,0:T(8,128)(2,1)S(1)} %bitcast.26) | data formatting | bytes 33554432
  30.3 137.1 %all-gather.5.cloned.1.call-done = bf16[26624,256]{1,0:T(8,128)(2,1)} async-done(((bf16[3328,256]{1,0:T(8,128)(2,1)}), bf16[26624,256]{1,0:T(8,128)(2,1)}) %all-gather.5.cloned.1.call-update) | async-done | bytes 13631504 | tf_op jit(solution)/shard_map/all_gather | solution.py:24
  167.5 141.4 %all-gather.3.cloned.1.call-done = bf16[512,26624]{1,0:T(8,128)(2,1)} async-done(((bf16[512,1664]{1,0:T(8,128)(2,1)}), bf16[512,26624]{1,0:T(8,128)(2,1)}) %all-gather.3.cloned.1.call-update) | async-done | bytes 27262992 | tf_op jit(solution)/shard_map/all_gather | solution.py:26
  308.9 16.4 %convolution_convert_fusion.2 = bf16[512,256]{1,0:T(8,128)(2,1)S(1)} fusion(bf16[512,26624]{1,0:T(8,128)(2,1)} %all-gather.3.cloned.1.call-done, bf16[26624,256]{1,0:T(8,128)(2,1)} %all-gather.5.cloned.1.call-done), kind=kOutput, calls=%fused_computation.4 | convolution fusion | flops 6979452928 | bytes 41156608 | tf_op jit(solution)/shard_map/dot_general | solution.py:25
  325.3 12.7 %convolution_convert_fusion.1 = bf16[256,16384]{1,0:T(8,128)(2,1)} fusion(bf16[512,256]{1,0:T(8,128)(2,1)S(1)} %convolution_convert_fusion.2, bf16[512,16384]{1,0:T(8,128)(2,1)} %bitcast.25), kind=kOutput, calls=%fused_computation.1 | convolution fusion | flops 4299161600 | bytes 25427968 | tf_op jit(solution)/shard_map/dot_general | solution.py:38
  338.0 9.4 %copy.20 = bf16[32,8,64,256]{3,2,1,0:T(8,128)(2,1)} copy(bf16[32,8,64,256]{3,1,2,0:T(8,128)(2,1)} %bitcast.29) | data formatting | bytes 16777216
  347.4 0.0 all-reduce.3.cloned.1.call-update
  347.5 0.6 copy-done.2
  348.1 0.1 dynamic-slice_convert_fusion
  348.2 0.1 broadcast_in_dim.16
  348.3 0.1 convert_element_type.51
  348.4 0.1 copy.17
  348.5 0.6 dynamic-slice
  349.7 7.2 broadcast_multiply_fusion.1
  356.9 9.4 %convolution_convert_fusion = bf16[16384,256]{1,0:T(8,128)(2,1)} fusion(bf16[16384,256]{1,0:T(8,128)(2,1)} %bitcast.28, bf16[256,256]{1,0:T(8,128)(2,1)S(1)} %copy-done), kind=kOutput, calls=%fused_computation | convolution fusion | flops 2151677952 | bytes 16908288 | tf_op jit(solution)/shard_map/dot_general | solution.py:49
  366.3 323.4 %all-reduce.3.cloned.1.call-done = bf16[256,64,256]{2,1,0:T(8,128)(2,1)} async-done(((bf16[256,64,256]{2,1,0:T(8,128)(2,1)}), bf16[256,64,256]{2,1,0:T(8,128)(2,1)}) %all-reduce.3.cloned.1.call-update) | async-done | bytes 8388624 | tf_op jit(solution)/shard_map/psum | solution.py:48
  689.7 5.5 constant_dynamic-slice_fusion
  695.2 5.6 copy.18
  700.8 8.1 %fusion = f32[64,64]{0,1:T(8,128)S(1)} fusion(bf16[256,64,256]{2,1,0:T(8,128)(2,1)} %all-reduce.3.cloned.1.call-done, bf16[256,64,256]{2,1,0:T(8,128)(2,1)} %bitcast.27), kind=kOutput, calls=%fused_computation.6 | convolution fusion | flops 536875008 | bytes 16793600 | tf_op jit(solution)/shard_map/dot_general | solution.py:51
  708.9 51.4 %all-reduce = f32[64,64]{0,1:T(8,128)S(1)} all-reduce(f32[64,64]{0,1:T(8,128)S(1)} %fusion), channel_id=2, replica_groups=mesh['row'=8,'col'=16] {'col'}, use_global_device_ids=true, to_apply=%region_1.0.clone | all-reduce | flops 4096 | bytes 32768
  760.4 0.7 dynamic_slice.15
  (8 shorter events, 0.1 us)
Async XLA Ops:
  7.2 349.8 %copy-start = (bf16[256,256]{1,0:T(8,128)(2,1)S(1)}, bf16[256,256]{1,0:T(8,128)(2,1)}, u32[]{:S(2)}) copy-start(bf16[256,256]{1,0:T(8,128)(2,1)} %param.11) | copy-start | bytes 393220
  7.2 160.3 %all-gather.5.cloned.1.call-start = ((), (), s32[]{:S(2)}) async-start(), calls=%async_computation.1 | async-start | bytes 15335424 | tf_op jit(solution)/shard_map/all_gather | solution.py:24
  7.9 300.9 %all-gather.3.cloned.1.call-start = ((), (), s32[]{:S(2)}) async-start(), calls=%async_computation | async-start | bytes 28966912 | tf_op jit(solution)/shard_map/all_gather | solution.py:26
  8.7 681.1 %all-reduce.3.cloned.1.call-start = ((), (), s32[]{:S(2)}) async-start(), calls=%async_computation.2 | async-start | bytes 16777216 | tf_op jit(solution)/shard_map/psum | solution.py:48
  325.3 12.8 %copy-start.1 = (bf16[512,256]{1,0:T(8,128)(2,1)}, bf16[512,256]{1,0:T(8,128)(2,1)S(1)}, u32[]{:S(2)}) copy-start(bf16[512,256]{1,0:T(8,128)(2,1)S(1)} %convolution_convert_fusion.2) | copy-start | bytes 786436
  347.4 0.7 copy-start.2
  347.4 1.1 copy-start.3
Sparse Core Ops, SparseCore 0:
  10.3 157.0 all-gather.4
  169.1 139.6 all-gather.2
  347.6 342.1 all-reduce.2
where the time goes:
time: 771 us; the launch traced here: 768 us
  waiting for transfers between devices  603 us (78%)
  blocking collectives  51.4 us (7%)
  matrix products  46.6 us (6%)
  local copies, waits for them, and re-layouts  35.5 us (5%)
  other arithmetic  16 us (2%)
  between operations  14.5 us (2%)
    psum x1, waiting for transfers between devices, per_device(): contracted = lax.psum(contract_part.astype(jnp.bfloat16), 'row')  323 us
    all_gather x1, waiting for transfers between devices, per_device(): lax.all_gather(polarization, 'col', axis=1, tiled=True)  141 us
    all_gather x1, waiting for transfers between devices, per_device(): metric_full = lax.all_gather(metric, 'row', axis=0, tiled=True)  137 us
    unnamed x1, blocking collectives  51.4 us
    unnamed x12, local copies, waits for them, and re-layouts  28.7 us
    dot_general x1, matrix products, per_device(): jnp.dot(lax.all_gather(polarization, 'col', axis=1, tiled=True), metric_f...  16.4 us
  transfers between devices with their start and end apart: 3, of which 3 were waited for; matrix products, arithmetic and copies ran while one was open for 5% of the time, Pallas kernels for 0%

commit v1 on v0

--- a/solution.py
+++ b/solution.py
@@ -1,16 +1,324 @@
+import functools
+
 import jax
 import jax.numpy as jnp
 from jax import lax
+from jax.experimental import pallas as pl
+from jax.experimental.pallas import tpu as pltpu
 from jax.sharding import PartitionSpec as P
 
 TILE = 64
 NL = 256
 RB = 64
 AB = 32
+MESH = pl.DeviceIdType.MESH
 
 
 def expand_mask(mask, rows, cols):
     return jnp.repeat(jnp.repeat(mask, rows, axis=0), cols, axis=1)
+
+
+def place():
+    row, col = lax.axis_index("row"), lax.axis_index("col")
+    return row // 2, row % 2, col // 4, (col // 2) % 2, col % 2
+
+
+def device(y, xh, z, xl, core):
+    return (y * 2 + xh, (z * 2 + xl) * 2 + core)
+
+
+class Copies:
+    def __init__(self, send_sem):
+        self.send_sem, self.started = send_sem, []
+
+    def send(self, src, dst, recv_sem, target):
+        index = len(self.started)
+        copy = pltpu.make_async_remote_copy(
+            src_ref=src,
+            dst_ref=dst,
+            send_sem=self.send_sem.at[index],
+            recv_sem=recv_sem,
+            device_id=target,
+            device_id_type=MESH,
+        )
+        copy.start()
+        self.started.append((copy, None))
+
+    def send_or_keep(self, keep, src, dst, recv_sem, target):
+        index = len(self.started)
+        copy = pltpu.make_async_remote_copy(
+            src_ref=src,
+            dst_ref=dst,
+            send_sem=self.send_sem.at[index],
+            recv_sem=recv_sem,
+            device_id=target,
+            device_id_type=MESH,
+        )
+
+        @pl.when(jnp.logical_not(keep))
+        def _():
+            copy.start()
+
+        @pl.when(keep)
+        def _():
+            pltpu.make_async_copy(src, dst, recv_sem).start()
+
+        self.started.append((copy, keep))
+
+    def finish(self):
+        for copy, keep in self.started:
+            if keep is None:
+                copy.wait_send()
+            else:
+                pl.when(jnp.logical_not(keep))(copy.wait_send)
+
+
+def landed(ref, sem):
+    pltpu.make_async_copy(ref, ref, sem).wait()
+
+
+def screen_kernel(
+    a_ref,
+    b_ref,
+    out_ref,
+    a0,
+    a1,
+    b0,
+    b1,
+    a1_own,
+    total,
+    give,
+    take,
+    send_sem,
+    local_sem,
+    x_sem,
+    near_sem,
+    far_sem,
+    twin_sem,
+    last_sem,
+):
+    y, xh, z, xl, core = place()
+    twin = device(y, xh, z, xl, 1 - core)
+    x = xh * 2 + xl
+    rows, depth = a_ref.shape
+    half, piece = rows // 2, rows // 4
+    cols = b_ref.shape[1]
+    z_at = [lax.rem(z + d, 4) for d in range(4)]
+    y_at = [lax.rem(y + d, 4) for d in range(4)]
+
+    barrier = pltpu.get_barrier_semaphore()
+    partners = [twin]
+    partners += [device(y, xh, z_at[d], xl, core) for d in (1, 3)]
+    partners += [device(y_at[d], xh, z, xl, core) for d in (1, 3)]
+    for d in (1, 2, 3):
+        other = lax.rem(x + d, 4)
+        partners.append(device(y, other // 2, z, other % 2, core))
+    for partner in partners:
+        pl.semaphore_signal(barrier, inc=1, device_id=partner, device_id_type=MESH)
+    pl.semaphore_wait(barrier, len(partners))
+
+    copies = Copies(send_sem)
+    first, second = pl.ds(0, depth), pl.ds(depth, depth)
+
+    own0, own1 = pl.ds(0, half), pl.ds(half, half)
+
+    @pl.when(core == 0)
+    def _():
+        pltpu.make_async_copy(a_ref, a0.at[z], local_sem.at[0]).start()
+        copy = pltpu.make_async_remote_copy(
+            a_ref, a0.at[z], send_sem.at[62], local_sem.at[0], device_id=twin, device_id_type=MESH
+        )
+        copy.start()
+
+    @pl.when(core == 1)
+    def _():
+        pltpu.make_async_copy(a_ref.at[own1], a1_own, local_sem.at[1]).start()
+        copy = pltpu.make_async_remote_copy(
+            a_ref.at[own0], a1_own, send_sem.at[62], local_sem.at[1], device_id=twin, device_id_type=MESH
+        )
+        copy.start()
+
+    for j in range(2):
+        keep = jnp.logical_and(j == xh, xh == xl)
+        copies.send_or_keep(
+            keep, b_ref.at[first], b0.at[y, xl], x_sem.at[2 + xl], device(y, j, z, xh, core)
+        )
+    b_own = pltpu.make_async_copy(b_ref.at[second], b1.at[y], local_sem.at[2])
+    b_own.start()
+
+    deep = depth // 2
+    b_up = [device(y_at[1], xh, z, xl, core), device(y_at[3], xh, z, xl, core)]
+    a_up = [device(y, xh, z_at[1], xl, core), device(y, xh, z_at[3], xl, core)]
+
+    def b_slot(stream, k, p):
+        buffer = b1.at[k] if stream == 0 else b0.at[k, stream - 1]
+        return buffer.at[pl.ds(p * deep, deep)]
+
+    def a_rows(stream, k, start, count):
+        buffer = a0.at[k] if stream == 0 else a1.at[k, stream - 1]
+        return buffer.at[pl.ds(pl.multiple_of(core * half + start, piece), count)]
+
+    def a_slot(stream, k, p):
+        return a_rows(stream, k, p * piece, piece)
+
+    def spread(slot, sem_base, stream, k, to):
+        for p in range(2):
+            for side in range(2):
+                q = p if side == 0 else 1 - p
+                copies.send(
+                    slot(stream, k, q), slot(stream, k, q), near_sem.at[sem_base + stream, side, q], to[side]
+                )
+
+    def go_on(slot, sem_base, stream, at, to):
+        for side in range(2):
+            k = at[3] if side == 0 else at[1]
+            landed(slot(stream, k, side), near_sem.at[sem_base + stream, side, side])
+            copies.send(
+                slot(stream, k, side), slot(stream, k, side), far_sem.at[sem_base + stream, side], to[side]
+            )
+
+    def to_twin(stream, k, index):
+        copies.send(
+            a_rows(stream, k, 0, half), a_rows(stream, k, 0, half), twin_sem.at[stream, index], twin
+        )
+
+    for p in range(2):
+        for side in range(2):
+            q = p if side == 0 else 1 - p
+            copies.send(
+                b_ref.at[pl.ds(depth + q * deep, deep)], b_slot(0, y, q), near_sem.at[3, side, q], b_up[side]
+            )
+
+    landed(a1_own, local_sem.at[1])
+    for j in range(2):
+        keep = jnp.logical_and(j == xl, xh == xl)
+        copies.send_or_keep(
+            keep, a1_own, a_rows_at(a1, z, xh, core, half), x_sem.at[xh], device(y, xl, z, j, core)
+        )
+    landed(a0.at[z], local_sem.at[0])
+    spread(a_slot, 0, 0, z, a_up)
+
+    go_on(b_slot, 3, 0, y_at, b_up)
+    go_on(a_slot, 0, 0, z_at, a_up)
+
+    for s in (1, 2):
+        landed(a_rows(s, z, 0, half), x_sem.at[s - 1])
+        spread(a_slot, 0, s, z, a_up)
+        landed(b0.at[y, s - 1], x_sem.at[1 + s])
+        spread(b_slot, 3, s, y, b_up)
+        to_twin(s, z, 3)
+
+    def rest(slot, sem_base, stream, at, side):
+        k = at[3] if side == 0 else at[1]
+        landed(slot(stream, k, 1 - side), near_sem.at[sem_base + stream, side, 1 - side])
+
+    for side in range(2):
+        rest(b_slot, 3, 0, y_at, side)
+        rest(a_slot, 0, 0, z_at, side)
+        to_twin(0, z_at[3] if side == 0 else z_at[1], side)
+    for s in (1, 2):
+        go_on(a_slot, 0, s, z_at, a_up)
+        go_on(b_slot, 3, s, y_at, b_up)
+
+    def far(slot, sem_base, stream, at):
+        for side in range(2):
+            landed(slot(stream, at[2], side), far_sem.at[sem_base + stream, side])
+
+    far(b_slot, 3, 0, y_at)
+    far(a_slot, 0, 0, z_at)
+    to_twin(0, z_at[2], 2)
+    for s in (1, 2):
+        for side in range(2):
+            rest(a_slot, 0, s, z_at, side)
+            rest(b_slot, 3, s, y_at, side)
+            to_twin(s, z_at[3] if side == 0 else z_at[1], side)
+    for s in (1, 2):
+        far(a_slot, 0, s, z_at)
+        to_twin(s, z_at[2], 2)
+        far(b_slot, 3, s, y_at)
+
+    def other_half(stream, k, index):
+        buffer = a0.at[k] if stream == 0 else a1.at[k, stream - 1]
+        start = pl.multiple_of((1 - core) * half, half)
+        landed(buffer.at[pl.ds(start, half)], twin_sem.at[stream, index])
+
+    for index, k in ((0, z_at[3]), (1, z_at[1]), (2, z_at[2])):
+        other_half(0, k, index)
+    for s in (1, 2):
+        for index, k in ((0, z_at[3]), (1, z_at[1]), (2, z_at[2]), (3, z)):
+            other_half(s, k, index)
+    b_own.wait()
+
+    def multiply(index, left, right):
+        def body(k, carry):
+            partial = jnp.dot(left(k)[...], right(k)[...], preferred_element_type=jnp.float32)
+            total[index] = jnp.where(k == 0, partial, total[index] + partial)
+            return carry
+
+        lax.fori_loop(0, 4, body, 0)
+
+    multiply(0, lambda k: a0.at[k], lambda k: b0.at[k, 1 - xl])
+    give[0] = total[0].astype(jnp.bfloat16)
+    copies.send(give.at[0], take.at[0], last_sem.at[0], device(y, xh, z, 1 - xl, core))
+    multiply(0, lambda k: a1.at[k, 1 - xh], lambda k: b1.at[k])
+    give[1] = total[0].astype(jnp.bfloat16)
+    copies.send(give.at[1], take.at[1], last_sem.at[1], device(y, 1 - xh, z, xl, core))
+    multiply(0, lambda k: a0.at[k], lambda k: b0.at[k, xl])
+    multiply(1, lambda k: a1.at[k, xh], lambda k: b1.at[k])
+    landed(take.at[0], last_sem.at[0])
+    landed(take.at[1], last_sem.at[1])
+    out_ref[...] = (
+        total[0] + total[1] + take[0].astype(jnp.float32) + take[1].astype(jnp.float32)
+    ).astype(jnp.bfloat16)
+
+    assert len(copies.started) <= 62
+    copies.finish()
+
+    @pl.when(core == 0)
+    def _():
+        pltpu.make_async_copy(a_ref, a0.at[z], send_sem.at[62]).wait()
+
+    @pl.when(core == 1)
+    def _():
+        pltpu.make_async_copy(a_ref.at[own0], a1_own, send_sem.at[62]).wait()
+
+
+def a_rows_at(a1, k, index, core, half):
+    return a1.at[k, index, pl.ds(pl.multiple_of(core * half, half), half)]
+
+
+def screen(a, b):
+    rows, depth = a.shape
+    cols = b.shape[1]
+    bf16 = jnp.bfloat16
+    dma = pltpu.SemaphoreType.DMA
+    return pl.pallas_call(
+        screen_kernel,
+        out_shape=jax.ShapeDtypeStruct((rows, cols), bf16),
+        in_specs=[pl.BlockSpec(memory_space=pl.ANY)] * 2,
+        out_specs=pl.BlockSpec(memory_space=pltpu.VMEM),
+        scratch_shapes=[
+            pltpu.VMEM((4, rows, depth), bf16),
+            pltpu.VMEM((4, 2, rows, depth), bf16),
+            pltpu.VMEM((4, 2, depth, cols), bf16),
+            pltpu.VMEM((4, depth, cols), bf16),
+            pltpu.VMEM((rows // 2, depth), bf16),
+            pltpu.VMEM((2, rows, cols), jnp.float32),
+            pltpu.VMEM((2, rows, cols), bf16),
+            pltpu.VMEM((2, rows, cols), bf16),
+            dma((64,)),
+            dma((3,)),
+            dma((4,)),
+            dma((6, 2, 2)),
+            dma((6, 2)),
+            dma((3, 4)),
+            dma((2,)),
+        ],
+        compiler_params=pltpu.CompilerParams(
+            collective_id=0, has_side_effects=True, vmem_limit_bytes=56 * 2**20
+        ),
+        name="screen",
+    )(a, b)
 
 
 def per_device(
@@ -21,13 +329,7 @@
     row_count = lax.axis_size("row")
     panel_rows = polarization.shape[0]
     near_cols = metric.shape[1]
-    metric_full = lax.all_gather(metric, "row", axis=0, tiled=True)
-    screened_sum = jnp.dot(
-        lax.all_gather(polarization, "col", axis=1, tiled=True),
-        metric_full,
-        preferred_element_type=jnp.float32,
-    )
-    screened = screened_sum.astype(jnp.bfloat16)
+    screened = screen(polarization, metric)
     panel_blocks = panel_rows // RB
     panel_mask = lax.dynamic_slice_in_dim(mask_panel, row_index * panel_blocks, panel_blocks, 0)
     panel = three_panel * expand_mask(panel_mask, RB, AB).astype(jnp.bfloat16)[:, None, :]

time: 771 us -> 613 us (0.80)
  waiting for transfers between devices: 603 us -> 318 us
  Pallas kernels: 0 us -> 141 us
  matrix products: 46.6 us -> 30.9 us
    all_gather x2 -> x0, waiting for transfers between devices: 279 us -> none  [the longest x1 141 us: per_device(): lax.all_gather(polarization, 'col', axis=1, tiled=True)]
    pallas_call x0 -> x1, Pallas kernels: none -> 141 us  [screen(): pl.pallas_call(screen_kernel, out_shape=jax.ShapeDtypeStruct((rows, cols)...]
    dot_general x1 -> x0, matrix products: 16.4 us -> none  [per_device(): jnp.dot(lax.all_gather(polarization, 'col', axis=1, tiled=True), metric_f...]
    unnamed x12 -> x13, local copies, waits for them, and re-layouts: 28.7 us -> 29.4 us
  transfers between devices with their start and end apart: 3 -> 1, of which waited for: 3 -> 1; matrix products, arithmetic and copies ran while one was open for 5% -> 3% of each run, Pallas kernels for 0% -> 0%
where the time goes in v1:
time: 613 us; the launch traced here: 610 us
  waiting for transfers between devices  318 us (52%)
  Pallas kernels  141 us (23%)
  blocking collectives  51.6 us (8%)
  local copies, waits for them, and re-layouts  36.1 us (6%)
  matrix products  30.9 us (5%)
  other arithmetic  16.7 us (3%)
  between operations  14.8 us (2%)
    psum x1, waiting for transfers between devices, per_device(): contracted = lax.psum(contract_part.astype(jnp.bfloat16), 'row')  318 us
    pallas_call x1, Pallas kernels, screen(): pl.pallas_call(screen_kernel, out_shape=jax.ShapeDtypeStruct((rows, cols)...  141 us
    unnamed x1, blocking collectives  51.6 us
    unnamed x13, local copies, waits for them, and re-layouts  29.4 us
    dot_general x1, matrix products, per_device(): lax.dot_general(screened, panel.reshape(panel_rows, TILE * NL), (((0,), (...  13.6 us
  transfers between devices with their start and end apart: 1, of which 1 were waited for; matrix products, arithmetic and copies ran while one was open for 3% of the time, Pallas kernels for 0%

profile of v1, /device:TPU:1, one launch (start us, length us, event | category | flops | bytes accessed | tf_op | source)
XLA Modules:
  0.0 609.8 jit_solution(17048772569430776305)
XLA Ops:
  7.2 0.0 copy-start
  7.2 0.0 all-reduce.3.cloned.1.call-start
  7.2 0.8 dynamic-slice_convert_fusion.1
  8.0 0.1 broadcast_in_dim.14
  8.1 0.1 convert_element_type.42
  8.2 0.1 copy.16
  8.3 8.0 %broadcast_multiply_fusion = bf16[512,64,256]{2,1,0:T(8,128)(2,1)S(1)} fusion(bf16[512,64,256]{2,1,0:T(8,128)(2,1)} %param.9, bf16[512,256]{1,0:T(8,128)(2,1)S(1)} %copy.16), kind=kLoop, calls=%fused_computation.2 | loop fusion | flops 8388608 | bytes 33816576 | tf_op jit(solution)/shard_map/mul | solution.py:335
  16.4 12.5 %copy.19 = bf16[64,8,64,256]{3,1,2,0:T(8,128)(2,1)} copy(bf16[64,8,64,256]{3,2,1,0:T(8,128)(2,1)S(1)} %bitcast.24) | data formatting | bytes 33554432
  28.8 141.2 %screen.1 = bf16[512,256]{1,0:T(8,128)(2,1)} custom-call(bf16[512,1664]{1,0:T(8,128)(2,1)} %a_ref.1, bf16[3328,256]{1,0:T(8,128)(2,1)} %b_ref.1), custom_call_target="tpu_custom_call" | custom-call | tf_op jit(solution)/shard_map/screen/pallas_call | solution.py:295
  170.0 13.6 %convolution_convert_fusion.1 = bf16[256,16384]{1,0:T(8,128)(2,1)} fusion(bf16[512,256]{1,0:T(8,128)(2,1)} %screen.1, bf16[512,16384]{1,0:T(8,128)(2,1)} %bitcast.23), kind=kOutput, calls=%fused_computation.1 | convolution fusion | flops 4299161600 | bytes 25427968 | tf_op jit(solution)/shard_map/dot_general | solution.py:340
  183.6 9.4 %copy.20 = bf16[32,8,64,256]{3,2,1,0:T(8,128)(2,1)} copy(bf16[32,8,64,256]{3,1,2,0:T(8,128)(2,1)} %bitcast.27) | data formatting | bytes 16777216
  193.0 0.0 copy-start.2
  193.0 0.0 all-reduce.3.cloned.1.call-update
  193.1 0.6 copy-done.2
  193.7 0.1 dynamic-slice_convert_fusion
  193.8 0.1 broadcast_in_dim.16
  193.8 0.1 convert_element_type.47
  194.0 0.1 copy.17
  194.1 0.0 copy-done.3
  194.1 0.6 dynamic-slice
  195.3 7.9 %broadcast_multiply_fusion.1 = bf16[256,64,256]{2,1,0:T(8,128)(2,1)} fusion(bf16[256,64,256]{2,1,0:T(8,128)(2,1)} %param.10, bf16[256,256]{1,0:T(8,128)(2,1)S(1)} %copy.17), kind=kLoop, calls=%fused_computation.3 | loop fusion | flops 4194304 | bytes 16908288 | tf_op jit(solution)/shard_map/mul | solution.py:338
  203.2 0.0 copy-done
  203.2 9.0 %convolution_convert_fusion = bf16[16384,256]{1,0:T(8,128)(2,1)} fusion(bf16[16384,256]{1,0:T(8,128)(2,1)} %bitcast.26, bf16[256,256]{1,0:T(8,128)(2,1)S(1)} %copy-done), kind=kOutput, calls=%fused_computation | convolution fusion | flops 2151677952 | bytes 16908288 | tf_op jit(solution)/shard_map/dot_general | solution.py:351
  212.2 318.4 %all-reduce.3.cloned.1.call-done = bf16[256,64,256]{2,1,0:T(8,128)(2,1)} async-done(((bf16[256,64,256]{2,1,0:T(8,128)(2,1)}), bf16[256,64,256]{2,1,0:T(8,128)(2,1)}) %all-reduce.3.cloned.1.call-update) | async-done | bytes 8388624 | tf_op jit(solution)/shard_map/psum | solution.py:350
  530.6 8.3 %fusion = f32[64,64]{0,1:T(8,128)S(1)} fusion(bf16[256,64,256]{2,1,0:T(8,128)(2,1)} %all-reduce.3.cloned.1.call-done, bf16[256,64,256]{2,1,0:T(8,128)(2,1)} %bitcast.25), kind=kOutput, calls=%fused_computation.5 | convolution fusion | flops 536875008 | bytes 16793600 | tf_op jit(solution)/shard_map/dot_general | solution.py:353
  538.9 0.0 copy-start.1
  538.9 51.6 %all-reduce = f32[64,64]{0,1:T(8,128)S(1)} all-reduce(f32[64,64]{0,1:T(8,128)S(1)} %fusion), channel_id=2, replica_groups=mesh['row'=8,'col'=16] {'col'}, use_global_device_ids=true, to_apply=%region_1.0.clone | all-reduce | flops 4096 | bytes 32768
  590.4 5.5 constant_dynamic-slice_fusion
  595.9 5.6 copy.18
  601.6 0.7 dynamic_slice.15
  602.2 0.0 copy-done.1
  602.2 0.7 copy.23
  (3 shorter events, 0.0 us)
Async XLA Ops:
  7.2 196.0 %copy-start = (bf16[256,256]{1,0:T(8,128)(2,1)S(1)}, bf16[256,256]{1,0:T(8,128)(2,1)}, u32[]{:S(2)}) copy-start(bf16[256,256]{1,0:T(8,128)(2,1)} %param.11) | copy-start | bytes 393220
  7.2 523.4 %all-reduce.3.cloned.1.call-start = ((), (), s32[]{:S(2)}) async-start(), calls=%async_computation | async-start | bytes 16777216 | tf_op jit(solution)/shard_map/psum | solution.py:350
  193.0 0.7 copy-start.2
  193.0 1.1 copy-start.3
  538.9 63.3 %copy-start.1 = (bf16[512,256]{1,0:T(8,128)(2,1)S(1)}, bf16[512,256]{1,0:T(8,128)(2,1)}, u32[]{:S(2)}) copy-start(bf16[512,256]{1,0:T(8,128)(2,1)} %screen.1) | copy-start | bytes 786436
Sparse Core Ops, SparseCore 0:
  193.2 337.3 all-reduce.2

commit v2 on v1

--- a/solution.py
+++ b/solution.py
@@ -77,10 +77,83 @@
     pltpu.make_async_copy(ref, ref, sem).wait()
 
 
+def prepare(panel, near, panel_mask, near_mask, green, panel_t, dressed, taken, flat, made, made_near, sem):
+    start = lambda k, size: pl.ds(pl.multiple_of(k * size, size), size)
+
+    def steps(source, mask, count, make, put, first, last):
+        def fetch(i):
+            block = source.at[start(i // 4, 128), start(i % 4, 16)]
+            return pltpu.make_async_copy(block, taken.at[i % 2], sem.at[i % 2])
+
+        fetch(first).start()
+
+        def body(i, carry):
+            @pl.when(i + 1 < last)
+            def _():
+                fetch(i + 1).start()
+
+            fetch(i).wait()
+
+            @pl.when(i >= first + 2)
+            def _():
+                put(i - 2).wait()
+
+            for h in range(2):
+                lanes = slice(h * 128, (h + 1) * 128)
+                flat[h] = taken[i % 2, :, :, lanes].astype(jnp.float32).reshape(128 * 16, 128)
+            rows = start(i // 4, 128)
+            for m in range(16):
+                make(
+                    i,
+                    m,
+                    [
+                        flat[h, pl.ds(m, 128, stride=16), :] * mask[rows, h * 128 : (h + 1) * 128]
+                        for h in range(2)
+                    ],
+                )
+            put(i).start()
+            return carry
+
+        lax.fori_loop(first, last, body, 0)
+        put(last - 2).wait()
+        put(last - 1).wait()
+
+    def put_panel(i):
+        place_at = panel_t.at[:, start(i % 4, 512), start(i // 4, 128)]
+        return pltpu.make_async_copy(made.at[i % 2], place_at, sem.at[2 + i % 2])
+
+    def put_near(i):
+        place_at = dressed.at[start(i % 4, 512), start(i // 4, 128)]
+        return pltpu.make_async_copy(made_near.at[i % 2], place_at, sem.at[2 + i % 2])
+
+    def make_panel(i, m, halves):
+        turned = jnp.concatenate([half.T.astype(jnp.bfloat16) for half in halves], 0)
+        made[i % 2, :, m * 32 : (m + 1) * 32, :] = turned.reshape(8, 32, 128)
+
+    def make_near(i, m, halves):
+        block = jnp.concatenate([half.astype(jnp.bfloat16) for half in halves], 1)
+        product = lax.dot_general(
+            green[...], block, (((1,), (1,)), ((), ())), preferred_element_type=jnp.float32
+        )
+        made_near[i % 2, m * 32 : (m + 1) * 32, :] = product.astype(jnp.bfloat16)
+
+    return (
+        functools.partial(steps, panel, panel_mask, 16, make_panel, put_panel),
+        functools.partial(steps, near, near_mask, 8, make_near, put_near),
+    )
+
+
 def screen_kernel(
     a_ref,
     b_ref,
+    panel,
+    near,
+    panel_mask,
+    near_mask,
+    green,
     out_ref,
+    panel_t,
+    dressed,
     a0,
     a1,
     b0,
@@ -89,6 +162,10 @@
     total,
     give,
     take,
+    taken,
+    flat,
+    made,
+    made_near,
     send_sem,
     local_sem,
     x_sem,
@@ -96,7 +173,11 @@
     far_sem,
     twin_sem,
     last_sem,
+    step_sem,
 ):
+    panel_steps, near_steps = prepare(
+        panel, near, panel_mask, near_mask, green, panel_t, dressed, taken, flat, made, made_near, step_sem
+    )
     y, xh, z, xl, core = place()
     twin = device(y, xh, z, xl, 1 - core)
     x = xh * 2 + xl
@@ -198,8 +279,10 @@
     landed(a0.at[z], local_sem.at[0])
     spread(a_slot, 0, 0, z, a_up)
 
+    panel_steps(0, 6)
     go_on(b_slot, 3, 0, y_at, b_up)
     go_on(a_slot, 0, 0, z_at, a_up)
+    panel_steps(6, 16)
 
     for s in (1, 2):
         landed(a_rows(s, z, 0, half), x_sem.at[s - 1])
@@ -207,6 +290,8 @@
         landed(b0.at[y, s - 1], x_sem.at[1 + s])
         spread(b_slot, 3, s, y, b_up)
         to_twin(s, z, 3)
+
+    near_steps(0, 8)
 
     def rest(slot, sem_base, stream, at, side):
         k = at[3] if side == 0 else at[1]
@@ -287,16 +372,21 @@
     return a1.at[k, index, pl.ds(pl.multiple_of(core * half, half), half)]
 
 
-def screen(a, b):
+def screen(a, b, panel, near, panel_mask, near_mask, green):
     rows, depth = a.shape
     cols = b.shape[1]
     bf16 = jnp.bfloat16
     dma = pltpu.SemaphoreType.DMA
+    hbm, vmem = pl.BlockSpec(memory_space=pl.ANY), pl.BlockSpec(memory_space=pltpu.VMEM)
     return pl.pallas_call(
         screen_kernel,
-        out_shape=jax.ShapeDtypeStruct((rows, cols), bf16),
-        in_specs=[pl.BlockSpec(memory_space=pl.ANY)] * 2,
-        out_specs=pl.BlockSpec(memory_space=pltpu.VMEM),
+        out_shape=(
+            jax.ShapeDtypeStruct((rows, cols), bf16),
+            jax.ShapeDtypeStruct((8, TILE * 32, rows), bf16),
+            jax.ShapeDtypeStruct((TILE * 32, cols), bf16),
+        ),
+        in_specs=[hbm] * 4 + [vmem] * 3,
+        out_specs=(vmem, hbm, hbm),
         scratch_shapes=[
             pltpu.VMEM((4, rows, depth), bf16),
             pltpu.VMEM((4, 2, rows, depth), bf16),
@@ -306,6 +396,10 @@
             pltpu.VMEM((2, rows, cols), jnp.float32),
             pltpu.VMEM((2, rows, cols), bf16),
             pltpu.VMEM((2, rows, cols), bf16),
+            pltpu.VMEM((2, 128, 16, NL), bf16),
+            pltpu.VMEM((2, 128 * 16, 128), jnp.float32),
+            pltpu.VMEM((2, 8, 16 * 32, 128), bf16),
+            pltpu.VMEM((2, 16 * 32, 128), bf16),
             dma((64,)),
             dma((3,)),
             dma((4,)),
@@ -313,12 +407,244 @@
             dma((6, 2)),
             dma((3, 4)),
             dma((2,)),
+            dma((4,)),
         ],
         compiler_params=pltpu.CompilerParams(
             collective_id=0, has_side_effects=True, vmem_limit_bytes=56 * 2**20
         ),
         name="screen",
-    )(a, b)
+    )(a, b, panel, near, panel_mask, near_mask, green)
+
+
+LATE = 1152
+
+
+def contract_kernel(
+    s_ref,
+    panel_t,
+    dressed,
+    out_ref,
+    energy_ref,
+    block,
+    part,
+    far_y,
+    near_y,
+    cross_y,
+    cross_x,
+    far_x,
+    near_x,
+    total,
+    other,
+    dressed_b,
+    tile,
+    row_sum,
+    tile_row,
+    tile_col,
+    send_sem,
+    block_sem,
+    far_sem,
+    near_sem,
+    cross_sem,
+    row_sem,
+    col_sem,
+):
+    y, xh, z, xl, core = place()
+    col = (z * 2 + xl) * 2 + core
+    f32, bf16 = jnp.float32, jnp.bfloat16
+
+    def in_row(d, j):
+        return device(lax.rem(y + d, 4), lax.rem(xh + j, 2), z, xl, core)
+
+    def in_col(d):
+        return (y * 2 + xh, lax.rem(col + d, 16))
+
+    partners = [in_row(s // 2, s % 2) for s in range(1, 8)] + [in_col(d) for d in range(1, 16)]
+    barrier = pltpu.get_barrier_semaphore()
+    for partner in partners:
+        pl.semaphore_signal(barrier, inc=1, device_id=partner, device_id_type=MESH)
+
+    order = [(2, 1), (2, 0), (1, 1), (3, 1), (1, 0), (3, 0), (0, 1), (0, 0)]
+
+    def fetch(i):
+        d, j = order[i]
+        share = lax.rem(y + d, 4) * 2 + lax.rem(xh + j, 2)
+        return pltpu.make_async_copy(panel_t.at[share], block.at[i % 2], block_sem.at[i % 2])
+
+    fetch(0).start()
+    dressed_copy = pltpu.make_async_copy(dressed, dressed_b, block_sem.at[2])
+    dressed_copy.start()
+    pl.semaphore_wait(barrier, len(partners))
+
+    copies = Copies(send_sem)
+    rows = TILE * 32
+    early = rows - LATE
+    h_late, h_early = LATE // 2, early // 2
+    up, down, across = in_row(1, 0), in_row(3, 0), in_row(0, 1)
+
+    def late(d, j, start=0, count=LATE):
+        return part.at[d * 2 + j, pl.ds(start, count)]
+
+    def first(d, j, start=0, count=early):
+        return part.at[d * 2 + j, pl.ds(LATE + start, count)]
+
+    for i, (d, j) in enumerate(order):
+        if i + 1 < 8:
+            fetch(i + 1).start()
+        fetch(i).wait()
+
+        def multiply(t, carry):
+            at = pl.ds(pl.multiple_of(t * 256, 256), 256)
+            part[d * 2 + j, at] = jnp.dot(
+                block[i % 2, at], s_ref[...], preferred_element_type=f32
+            ).astype(bf16)
+            return carry
+
+        lax.fori_loop(0, rows // 256, multiply, 0)
+        if j == 1:
+            copies.send(first(d, 1), cross_x.at[d], cross_sem.at[d], across)
+        if d == 2:
+            copies.send(late(2, j, 0, h_late), far_y.at[j, 0], far_sem.at[j, 0], up)
+            copies.send(late(2, j, h_late, h_late), far_y.at[j, 1], far_sem.at[j, 1], down)
+        if d == 1:
+            copies.send(late(1, j, h_late, h_late), near_y.at[j, 0, pl.ds(h_late, h_late)], near_sem.at[j, 0, 0], up)
+        if d == 3:
+            copies.send(late(3, j, 0, h_late), near_y.at[j, 1, pl.ds(0, h_late)], near_sem.at[j, 1, 0], down)
+
+    def add(ref, *others):
+        result = ref[...].astype(f32)
+        for each in others:
+            result = result + each[...].astype(f32)
+        ref[...] = result.astype(bf16)
+
+    for j in (1, 0):
+        landed(far_y.at[j, 0], far_sem.at[j, 0])
+        add(late(1, j, 0, h_late), far_y.at[j, 0])
+        copies.send(late(1, j, 0, h_late), near_y.at[j, 0, pl.ds(0, h_late)], near_sem.at[j, 0, 1], up)
+        landed(far_y.at[j, 1], far_sem.at[j, 1])
+        add(late(3, j, h_late, h_late), far_y.at[j, 1])
+        copies.send(late(3, j, h_late, h_late), near_y.at[j, 1, pl.ds(h_late, h_late)], near_sem.at[j, 1, 1], down)
+
+    landed(cross_x.at[2], cross_sem.at[2])
+    add(first(2, 0), cross_x.at[2])
+    copies.send(first(2, 0, 0, h_early), far_x.at[0], far_sem.at[2, 0], up)
+    copies.send(first(2, 0, h_early, h_early), far_x.at[1], far_sem.at[2, 1], down)
+    landed(cross_x.at[1], cross_sem.at[1])
+    add(first(1, 0), cross_x.at[1])
+    copies.send(first(1, 0, h_early, h_early), near_x.at[0, pl.ds(h_early, h_early)], near_sem.at[2, 0, 0], up)
+    landed(cross_x.at[3], cross_sem.at[3])
+    add(first(3, 0), cross_x.at[3])
+    copies.send(first(3, 0, 0, h_early), near_x.at[1, pl.ds(0, h_early)], near_sem.at[2, 1, 0], down)
+
+    def both_near(j, ref):
+        count = ref.shape[1] // 2
+        for side in range(2):
+            for turn in range(2):
+                start = count if (side == 0) == (turn == 0) else 0
+                landed(ref.at[side, pl.ds(start, count)], near_sem.at[j, side, turn])
+
+    both_near(1, near_y.at[1])
+    add(late(0, 1), near_y.at[1, 0], near_y.at[1, 1])
+    copies.send(late(0, 1), cross_y, cross_sem.at[4], across)
+
+    landed(far_x.at[0], far_sem.at[2, 0])
+    add(first(1, 0, 0, h_early), far_x.at[0])
+    copies.send(first(1, 0, 0, h_early), near_x.at[0, pl.ds(0, h_early)], near_sem.at[2, 0, 1], up)
+    landed(far_x.at[1], far_sem.at[2, 1])
+    add(first(3, 0, h_early, h_early), far_x.at[1])
+    copies.send(first(3, 0, h_early, h_early), near_x.at[1, pl.ds(h_early, h_early)], near_sem.at[2, 1, 1], down)
+
+    dressed_copy.wait()
+    for h in range(2):
+        other[h] = dressed_b[:, h * 128 : (h + 1) * 128].astype(f32)
+
+    def settle(at, *terms):
+        result = terms[0][...].astype(f32)
+        for each in terms[1:]:
+            result = result + each[...].astype(f32)
+        result = result.astype(bf16)
+        out_ref[at] = result
+        for h in range(2):
+            total[h, at] = result[:, h * 128 : (h + 1) * 128].astype(f32)
+
+    both_near(0, near_y.at[0])
+    landed(cross_x.at[0], cross_sem.at[0])
+    landed(cross_y, cross_sem.at[4])
+    settle(pl.ds(0, LATE), late(0, 0), near_y.at[0, 0], near_y.at[0, 1], cross_y)
+    both_near(2, near_x)
+    settle(pl.ds(LATE, early), first(0, 0), cross_x.at[0], near_x.at[0], near_x.at[1])
+
+    def column(ref, l):
+        halves = [ref[h, pl.ds(l, TILE, stride=32), :].astype(bf16) for h in range(2)]
+        return jnp.concatenate(halves, 1)
+
+    energy = jnp.zeros((TILE, TILE), f32)
+    for l in range(32):
+        energy = energy + lax.dot_general(
+            column(total, l), column(other, l), (((1,), (1,)), ((), ())), preferred_element_type=f32
+        )
+    tile[...] = jnp.concatenate([-energy, jnp.zeros_like(energy)], 1)
+
+    def share_of(row):
+        return pl.ds(pl.multiple_of(row * 8, 8), 8)
+
+    for s in range(1, 8):
+        target = in_row(s // 2, s % 2)
+        copies.send(tile.at[share_of(target[0])], tile_row.at[s], row_sem.at[s], target)
+    mine = tile[share_of(y * 2 + xh)]
+    for s in range(1, 8):
+        landed(tile_row.at[s], row_sem.at[s])
+        mine = mine + tile_row[s]
+    row_sum[...] = mine
+    for d in range(1, 16):
+        copies.send(row_sum, tile_col.at[d], col_sem.at[d], in_col(d))
+    for d in range(1, 16):
+        landed(tile_col.at[d], col_sem.at[d])
+        mine = mine + tile_col[d]
+    energy_ref[...] = mine
+    copies.finish()
+
+
+def contract(screened, panel_t, dressed):
+    rows = TILE * 32
+    cols = screened.shape[1]
+    early = rows - LATE
+    bf16, f32 = jnp.bfloat16, jnp.float32
+    dma = pltpu.SemaphoreType.DMA
+    hbm, vmem = pl.BlockSpec(memory_space=pl.ANY), pl.BlockSpec(memory_space=pltpu.VMEM)
+    return pl.pallas_call(
+        contract_kernel,
+        out_shape=(jax.ShapeDtypeStruct((rows, cols), bf16), jax.ShapeDtypeStruct((8, 128), f32)),
+        in_specs=[vmem, hbm, hbm],
+        out_specs=(vmem, vmem),
+        scratch_shapes=[
+            pltpu.VMEM((2, rows, screened.shape[0]), bf16),
+            pltpu.VMEM((8, rows, cols), bf16),
+            pltpu.VMEM((2, 2, LATE // 2, cols), bf16),
+            pltpu.VMEM((2, 2, LATE, cols), bf16),
+            pltpu.VMEM((LATE, cols), bf16),
+            pltpu.VMEM((4, early, cols), bf16),
+            pltpu.VMEM((2, early // 2, cols), bf16),
+            pltpu.VMEM((2, early, cols), bf16),
+            pltpu.VMEM((2, rows, 128), f32),
+            pltpu.VMEM((2, rows, 128), f32),
+            pltpu.VMEM((rows, cols), bf16),
+            pltpu.VMEM((TILE, 128), f32),
+            pltpu.VMEM((8, 128), f32),
+            pltpu.VMEM((8, 8, 128), f32),
+            pltpu.VMEM((16, 8, 128), f32),
+            dma((48,)),
+            dma((3,)),
+            dma((3, 2)),
+            dma((3, 2, 2)),
+            dma((5,)),
+            dma((8,)),
+            dma((16,)),
+        ],
+        compiler_params=pltpu.CompilerParams(
+            collective_id=1, has_side_effects=True, vmem_limit_bytes=56 * 2**20
+        ),
+        name="contract",
+    )(screened, panel_t, dressed)
 
 
 def per_device(
@@ -329,35 +655,25 @@
     row_count = lax.axis_size("row")
     panel_rows = polarization.shape[0]
     near_cols = metric.shape[1]
-    screened = screen(polarization, metric)
     panel_blocks = panel_rows // RB
     panel_mask = lax.dynamic_slice_in_dim(mask_panel, row_index * panel_blocks, panel_blocks, 0)
-    panel = three_panel * expand_mask(panel_mask, RB, AB).astype(jnp.bfloat16)[:, None, :]
     near_blocks = near_cols // RB
     near_mask = lax.dynamic_slice_in_dim(mask_near, col_index * near_blocks, near_blocks, 0)
-    near = three_near * expand_mask(near_mask, RB, AB).astype(jnp.bfloat16)[:, None, :]
-    near_flat = near.reshape(near_cols * TILE, NL)
-    contract_part = lax.dot_general(
-        screened,
-        panel.reshape(panel_rows, TILE * NL),
-        (((0,), (0,)), ((), ())),
-        preferred_element_type=jnp.float32,
+    near_share = NL // row_count
+    green = lax.dynamic_slice_in_dim(green_function, row_index * near_share, near_share, 0)
+    screened, panel_t, dressed = screen(
+        polarization,
+        metric,
+        three_panel,
+        three_near,
+        expand_mask(panel_mask, RB, AB).astype(jnp.float32),
+        expand_mask(near_mask, RB, AB).astype(jnp.float32),
+        green,
     )
-    contract_part = (
-        contract_part.astype(jnp.bfloat16).astype(jnp.float32).reshape(near_cols, TILE, NL)
-    )
-    near_share = NL // row_count
-    contracted = lax.psum(contract_part.astype(jnp.bfloat16), "row")
-    dressed = jnp.dot(near_flat, green_function.T, preferred_element_type=jnp.float32)
-    dressed = dressed.astype(jnp.bfloat16).reshape(near_cols, TILE, NL)
-    tile_part = -lax.dot_general(
-        contracted, dressed, (((0, 2), (0, 2)), ((), ())), preferred_element_type=jnp.float32
-    )
-    column_share = lax.psum_scatter(tile_part, "col", scatter_dimension=1, tiled=True)
-    row_share = TILE // row_count
-    self_energy = lax.dynamic_slice_in_dim(column_share, row_index * row_share, row_share, 0)
-    contracted_out = lax.dynamic_slice_in_dim(contracted, row_index * near_share, near_share, 2)
-    return (screened, contracted_out, self_energy)
+    contracted, energy = contract(screened, panel_t, dressed)
+    contracted = contracted.T.reshape(near_cols, TILE, near_share)
+    self_energy = lax.dynamic_slice_in_dim(energy, col_index * 4, 4, 1)
+    return (screened, contracted, self_energy)
 
 
 def solution(mesh):

time: 613 us -> 226 us (0.37)
  waiting for transfers between devices: 318 us -> 0 us
  Pallas kernels: 141 us -> 215 us
  blocking collectives: 51.6 us -> 0 us
  matrix products: 30.9 us -> 0 us
  local copies, waits for them, and re-layouts: 36.1 us -> 7.22 us
  other arithmetic: 16.7 us -> 1.56 us
  between operations: 14.8 us -> 0.69 us
    psum x1 -> x0, waiting for transfers between devices: 318 us -> none  [per_device(): contracted = lax.psum(contract_part.astype(jnp.bfloat16), 'row')]
    pallas_call x1 -> x2, Pallas kernels: 141 us -> 215 us  [the longest x1 142 us: screen(): pl.pallas_call(screen_kernel, out_shape=(jax.ShapeDtypeStruct((rows, cols...]
    unnamed x1 -> x0, blocking collectives: 51.6 us -> none
    dot_general x3 -> x0, matrix products: 30.9 us -> none  [the longest x1 13.6 us: per_device(): lax.dot_general(screened, panel.reshape(panel_rows, TILE * NL), (((0,), (...]
    unnamed x13 -> x7, local copies, waits for them, and re-layouts: 29.4 us -> 3.63 us
    mul x2 -> x0, other arithmetic: 15.9 us -> none  [the longest x1 8.01 us: per_device(): three_panel * expand_mask(panel_mask, RB, AB).astype(jnp.bfloat16)[:, Non...]
  transfers between devices with their start and end apart: 1 -> 0, of which waited for: 1 -> 0; matrix products, arithmetic and copies ran while one was open for 3% -> 0% of each run, Pallas kernels for 0% -> 0%
where the time goes in v2:
time: 226 us; the launch traced here: 225 us
  Pallas kernels  215 us (95%)
  local copies, waits for them, and re-layouts  7.22 us (3%)
    pallas_call x1, Pallas kernels, screen(): pl.pallas_call(screen_kernel, out_shape=(jax.ShapeDtypeStruct((rows, cols...  142 us
    pallas_call x1, Pallas kernels, contract(): pl.pallas_call(contract_kernel, out_shape=(jax.ShapeDtypeStruct((rows, co...  73.1 us

profile of v2, /device:TPU:1, one launch (start us, length us, event | category | flops | bytes accessed | tf_op | source)
XLA Modules:
  0.0 224.9 jit_solution(3832779395402105419)
XLA Ops:
  0.6 0.0 copy-start
  0.7 0.8 dynamic-slice_convert_fusion.1
  1.4 0.8 dynamic-slice_convert_fusion
  2.2 0.1 broadcast_in_dim.14
  2.3 0.1 convert_element_type.18
  2.4 0.0 copy-done
  2.4 0.6 constant_dynamic-slice_fusion.1.green
  3.0 0.1 broadcast_in_dim.12
  3.1 0.1 convert_element_type.15
  3.2 0.8 copy.14.near_mask
  4.1 1.0 copy.13.panel_mask
  5.1 142.3 %screen.1 = (bf16[512,256]{1,0:T(8,128)(2,1)}, bf16[8,2048,512]{2,1,0:T(8,128)(2,1)}, bf16[2048,256]{1,0:T(8,128)(2,1)}) custom-call(bf16[512,1664]{1,0:T(8,128)(2,1)} %a_ref.1, bf16[3328,256]{1,0:T(8,128)(2,1)} %b_ref.1, bf16[512,64,256]{2,1,0:T(8,128)(2,1)} %panel.1, bf16[256,64,256]{2,1,0:T(8,128)(2,1)} %near.1, f32[512,256]{1,0:T(8,128)} %copy.13.panel_mask, ...), custom_call_target="tpu_custom_call" | custom-call | tf_op jit(solution)/shard_map/screen/pallas_call | solution.py:381
  147.4 0.0 copy-start.1
  147.4 73.1 %contract.1 = (bf16[2048,256]{1,0:T(8,128)(2,1)}, f32[8,128]{1,0:T(8,128)}) custom-call(bf16[512,256]{1,0:T(8,128)(2,1)} %get-tuple-element.22.s_ref, bf16[8,2048,512]{2,1,0:T(8,128)(2,1)} %get-tuple-element.9.panel_t, bf16[2048,256]{1,0:T(8,128)(2,1)} %get-tuple-element.10.dressed), custom_call_target="tpu_custom_call" | custom-call | tf_op jit(solution)/shard_map/contract/pallas_call | solution.py:614
  220.5 0.8 constant_dynamic-slice_fusion
  221.3 0.7 copy.15
  221.9 0.0 copy-done.1
  221.9 0.7 copy.18
  222.6 2.3 %copy.19 = bf16[256,64,32]{0,2,1:T(8,128)(2,1)} copy(bf16[256,64,32]{0,2,1:T(8,128)(2,1)} %bitcast.10) | data formatting | bytes 2097152
  (2 shorter events, 0.1 us)
Async XLA Ops:
  0.6 1.7 copy-start
  147.4 74.5 %copy-start.1 = (bf16[512,256]{1,0:T(8,128)(2,1)S(1)}, bf16[512,256]{1,0:T(8,128)(2,1)}, u32[]{:S(2)}) copy-start(bf16[512,256]{1,0:T(8,128)(2,1)} %get-tuple-element.22.s_ref) | copy-start | bytes 786436

commit v3 on v2

--- a/solution.py
+++ b/solution.py
@@ -167,6 +167,7 @@
     made,
     made_near,
     send_sem,
+    own_sem,
     local_sem,
     x_sem,
     near_sem,
@@ -183,7 +184,6 @@
     x = xh * 2 + xl
     rows, depth = a_ref.shape
     half, piece = rows // 2, rows // 4
-    cols = b_ref.shape[1]
     z_at = [lax.rem(z + d, 4) for d in range(4)]
     y_at = [lax.rem(y + d, 4) for d in range(4)]
 
@@ -199,7 +199,6 @@
     pl.semaphore_wait(barrier, len(partners))
 
     copies = Copies(send_sem)
-    first, second = pl.ds(0, depth), pl.ds(depth, depth)
 
     own0, own1 = pl.ds(0, half), pl.ds(half, half)
 
@@ -207,7 +206,7 @@
     def _():
         pltpu.make_async_copy(a_ref, a0.at[z], local_sem.at[0]).start()
         copy = pltpu.make_async_remote_copy(
-            a_ref, a0.at[z], send_sem.at[62], local_sem.at[0], device_id=twin, device_id_type=MESH
+            a_ref, a0.at[z], own_sem, local_sem.at[0], device_id=twin, device_id_type=MESH
         )
         copy.start()
 
@@ -215,161 +214,202 @@
     def _():
         pltpu.make_async_copy(a_ref.at[own1], a1_own, local_sem.at[1]).start()
         copy = pltpu.make_async_remote_copy(
-            a_ref.at[own0], a1_own, send_sem.at[62], local_sem.at[1], device_id=twin, device_id_type=MESH
+            a_ref.at[own0], a1_own, own_sem, local_sem.at[1], device_id=twin, device_id_type=MESH
         )
         copy.start()
 
-    for j in range(2):
-        keep = jnp.logical_and(j == xh, xh == xl)
-        copies.send_or_keep(
-            keep, b_ref.at[first], b0.at[y, xl], x_sem.at[2 + xl], device(y, j, z, xh, core)
-        )
-    b_own = pltpu.make_async_copy(b_ref.at[second], b1.at[y], local_sem.at[2])
-    b_own.start()
-
-    deep = depth // 2
+    deep = (depth // 256 * 128 + 128, depth // 256 * 128)
+
+    def b_slot(stream, k, p, part=None):
+        buffer = b1.at[k] if stream == 0 else b0.at[k, stream - 1]
+        start, count = p * deep[0], deep[p]
+        if part is not None:
+            start, count = start + part * (count // 2), count // 2
+        return buffer.at[pl.ds(start, count)]
+
+    def a_rows(stream, k, start, count):
+        buffer = a0.at[k] if stream == 0 else a1.at[k, stream - 1]
+        return buffer.at[pl.ds(start, count)]
+
+    def a_slot(stream, k, p, part=None, of=core):
+        start, count = of * half + p * piece, piece
+        if part is not None:
+            start, count = start + part * (count // 2), count // 2
+        return a_rows(stream, k, pl.multiple_of(start, piece // 2), count)
+
     b_up = [device(y_at[1], xh, z, xl, core), device(y_at[3], xh, z, xl, core)]
     a_up = [device(y, xh, z_at[1], xl, core), device(y, xh, z_at[3], xl, core)]
-
-    def b_slot(stream, k, p):
-        buffer = b1.at[k] if stream == 0 else b0.at[k, stream - 1]
-        return buffer.at[pl.ds(p * deep, deep)]
-
-    def a_rows(stream, k, start, count):
-        buffer = a0.at[k] if stream == 0 else a1.at[k, stream - 1]
-        return buffer.at[pl.ds(pl.multiple_of(core * half + start, piece), count)]
-
-    def a_slot(stream, k, p):
-        return a_rows(stream, k, p * piece, piece)
-
-    def spread(slot, sem_base, stream, k, to):
-        for p in range(2):
+    A, B = (a_slot, 0, z_at, a_up), (b_slot, 3, y_at, b_up)
+
+    def b_own(p, base=0):
+        return b_ref.at[pl.ds(base + p * deep[0], deep[p])]
+
+    def b_along_x(p):
+        for j in range(2):
+            keep = jnp.logical_and(j == xh, xh == xl)
+            at = b0.at[y, xl, pl.ds(p * deep[0], deep[p])]
+            copies.send_or_keep(keep, b_own(p), at, x_sem.at[1, xl, p], device(y, j, z, xh, core))
+
+    def a_along_x(p):
+        for j in range(2):
+            keep = jnp.logical_and(j == xl, xh == xl)
+            at = a1.at[z, xh, pl.ds(pl.multiple_of(core * half + p * piece, piece), piece)]
+            source = a1_own.at[pl.ds(p * piece, piece)]
+            copies.send_or_keep(keep, source, at, x_sem.at[0, xh, p], device(y, xl, z, j, core))
+
+    def spread(array, stream, p, source=None):
+        slot, base, at, to = array
+        for side in range(2):
+            here = slot(stream, at[0], p)
+            copies.send(here if source is None else source, here, near_sem.at[base + stream, side, p], to[side])
+
+    def to_twin(stream, k, p, index):
+        here = a_slot(stream, k, p)
+        copies.send(here, here, twin_sem.at[stream, index, p], twin)
+
+    def go_on(array, stream, p):
+        slot, base, at, to = array
+        for side in range(2):
+            k = at[3 - 2 * side]
+            landed(slot(stream, k, p), near_sem.at[base + stream, side, p])
+            half_of = slot(stream, k, p, side)
+            copies.send(half_of, half_of, far_sem.at[base + stream, side, p], to[side])
+        if base == 0:
             for side in range(2):
-                q = p if side == 0 else 1 - p
-                copies.send(
-                    slot(stream, k, q), slot(stream, k, q), near_sem.at[sem_base + stream, side, q], to[side]
-                )
-
-    def go_on(slot, sem_base, stream, at, to):
+                to_twin(stream, at[3 - 2 * side], p, 3 - 2 * side)
+
+    def far(array, stream, p):
+        slot, base, at, to = array
         for side in range(2):
-            k = at[3] if side == 0 else at[1]
-            landed(slot(stream, k, side), near_sem.at[sem_base + stream, side, side])
-            copies.send(
-                slot(stream, k, side), slot(stream, k, side), far_sem.at[sem_base + stream, side], to[side]
+            landed(slot(stream, at[2], p, side), far_sem.at[base + stream, side, p])
+        if base == 0:
+            to_twin(stream, at[2], p, 2)
+
+    def from_twin(stream, p, indices):
+        for d in indices:
+            landed(a_slot(stream, z_at[d], p, of=1 - core), twin_sem.at[stream, d, p])
+
+    def arrive(p):
+        for s in (1, 2):
+            landed(a_slot(s, z, p), x_sem.at[0, s - 1, p])
+            spread(A, s, p)
+            to_twin(s, z, p, 0)
+            landed(b_slot(s, y, p), x_sem.at[1, s - 1, p])
+            spread(B, s, p)
+
+    def keep_rows(k, p, j):
+        lanes = slice(p * deep[0], p * deep[0] + deep[p])
+
+        def body(t, carry):
+            at = pl.ds(pl.multiple_of(t * half, half), half)
+            total[0, j, at] += jnp.dot(
+                a0[k, at, lanes], b0[k, j, lanes], preferred_element_type=jnp.float32
             )
-
-    def to_twin(stream, k, index):
-        copies.send(
-            a_rows(stream, k, 0, half), a_rows(stream, k, 0, half), twin_sem.at[stream, index], twin
-        )
-
+            return carry
+
+        lax.fori_loop(0, 2, body, 0)
+
+    def keep_cols(k, p, j):
+        def body(t, carry):
+            at = pl.ds(pl.multiple_of(t * half + p * piece, piece), piece)
+            total[1, j, at] += jnp.dot(a1[k, j, at], b1[k], preferred_element_type=jnp.float32)
+            return carry
+
+        lax.fori_loop(0, 2, body, 0)
+
+    def multiply(p, distances):
+        def body(j, carry):
+            for d in distances:
+                keep_rows(y_at[d], p, j)
+                keep_cols(z_at[d], p, j)
+            return carry
+
+        lax.fori_loop(0, 2, body, 0)
+
+    b_along_x(0)
+    b_local = pltpu.make_async_copy(b_ref.at[pl.ds(depth, depth)], b1.at[y], local_sem.at[2])
+    b_local.start()
     for p in range(2):
-        for side in range(2):
-            q = p if side == 0 else 1 - p
-            copies.send(
-                b_ref.at[pl.ds(depth + q * deep, deep)], b_slot(0, y, q), near_sem.at[3, side, q], b_up[side]
-            )
-
+        spread(B, 0, p, b_own(p, depth))
     landed(a1_own, local_sem.at[1])
-    for j in range(2):
-        keep = jnp.logical_and(j == xl, xh == xl)
-        copies.send_or_keep(
-            keep, a1_own, a_rows_at(a1, z, xh, core, half), x_sem.at[xh], device(y, xl, z, j, core)
-        )
+    a_along_x(0)
+    b_along_x(1)
+    a_along_x(1)
     landed(a0.at[z], local_sem.at[0])
-    spread(a_slot, 0, 0, z, a_up)
-
-    panel_steps(0, 6)
-    go_on(b_slot, 3, 0, y_at, b_up)
-    go_on(a_slot, 0, 0, z_at, a_up)
-    panel_steps(6, 16)
-
+    for p in range(2):
+        spread(A, 0, p)
+    total[...] = jnp.zeros_like(total)
+
+    panel_steps(0, 4)
+    go_on(B, 0, 0)
+    go_on(A, 0, 0)
+    panel_steps(4, 9)
+    go_on(B, 0, 1)
+    go_on(A, 0, 1)
+    panel_steps(9, 12)
+    arrive(0)
+    panel_steps(12, 16)
+    for p in range(2):
+        far(B, 0, p)
+        far(A, 0, p)
+    near_steps(0, 4)
+    go_on(A, 1, 0)
+    go_on(B, 1, 0)
+    near_steps(4, 8)
+    b_local.wait()
+    go_on(A, 2, 0)
+    go_on(B, 2, 0)
+    arrive(1)
+    for p in range(2):
+        from_twin(0, p, (1, 2, 3))
     for s in (1, 2):
-        landed(a_rows(s, z, 0, half), x_sem.at[s - 1])
-        spread(a_slot, 0, s, z, a_up)
-        landed(b0.at[y, s - 1], x_sem.at[1 + s])
-        spread(b_slot, 3, s, y, b_up)
-        to_twin(s, z, 3)
-
-    near_steps(0, 8)
-
-    def rest(slot, sem_base, stream, at, side):
-        k = at[3] if side == 0 else at[1]
-        landed(slot(stream, k, 1 - side), near_sem.at[sem_base + stream, side, 1 - side])
-
-    for side in range(2):
-        rest(b_slot, 3, 0, y_at, side)
-        rest(a_slot, 0, 0, z_at, side)
-        to_twin(0, z_at[3] if side == 0 else z_at[1], side)
+        from_twin(s, 0, (0, 1, 3))
+    multiply(0, (0, 1))
     for s in (1, 2):
-        go_on(a_slot, 0, s, z_at, a_up)
-        go_on(b_slot, 3, s, y_at, b_up)
-
-    def far(slot, sem_base, stream, at):
-        for side in range(2):
-            landed(slot(stream, at[2], side), far_sem.at[sem_base + stream, side])
-
-    far(b_slot, 3, 0, y_at)
-    far(a_slot, 0, 0, z_at)
-    to_twin(0, z_at[2], 2)
+        far(A, s, 0)
+        far(B, s, 0)
+    multiply(0, (3,))
+    go_on(A, 1, 1)
+    go_on(B, 1, 1)
     for s in (1, 2):
-        for side in range(2):
-            rest(a_slot, 0, s, z_at, side)
-            rest(b_slot, 3, s, y_at, side)
-            to_twin(s, z_at[3] if side == 0 else z_at[1], side)
+        from_twin(s, 0, (2,))
+        from_twin(s, 1, (0,))
+    multiply(0, (2,))
+    go_on(A, 2, 1)
+    go_on(B, 2, 1)
+    multiply(1, (0,))
     for s in (1, 2):
-        far(a_slot, 0, s, z_at)
-        to_twin(s, z_at[2], 2)
-        far(b_slot, 3, s, y_at)
-
-    def other_half(stream, k, index):
-        buffer = a0.at[k] if stream == 0 else a1.at[k, stream - 1]
-        start = pl.multiple_of((1 - core) * half, half)
-        landed(buffer.at[pl.ds(start, half)], twin_sem.at[stream, index])
-
-    for index, k in ((0, z_at[3]), (1, z_at[1]), (2, z_at[2])):
-        other_half(0, k, index)
+        from_twin(s, 1, (1, 3))
+    multiply(1, (1, 3))
     for s in (1, 2):
-        for index, k in ((0, z_at[3]), (1, z_at[1]), (2, z_at[2]), (3, z)):
-            other_half(s, k, index)
-    b_own.wait()
-
-    def multiply(index, left, right):
-        def body(k, carry):
-            partial = jnp.dot(left(k)[...], right(k)[...], preferred_element_type=jnp.float32)
-            total[index] = jnp.where(k == 0, partial, total[index] + partial)
-            return carry
-
-        lax.fori_loop(0, 4, body, 0)
-
-    multiply(0, lambda k: a0.at[k], lambda k: b0.at[k, 1 - xl])
-    give[0] = total[0].astype(jnp.bfloat16)
+        far(A, s, 1)
+        far(B, s, 1)
+    for s in (1, 2):
+        from_twin(s, 1, (2,))
+
+    keep_rows(y_at[2], 1, 1 - xl)
+    give[0] = total[0, 1 - xl].astype(jnp.bfloat16)
     copies.send(give.at[0], take.at[0], last_sem.at[0], device(y, xh, z, 1 - xl, core))
-    multiply(0, lambda k: a1.at[k, 1 - xh], lambda k: b1.at[k])
-    give[1] = total[0].astype(jnp.bfloat16)
+    keep_cols(z_at[2], 1, 1 - xh)
+    give[1] = total[1, 1 - xh].astype(jnp.bfloat16)
     copies.send(give.at[1], take.at[1], last_sem.at[1], device(y, 1 - xh, z, xl, core))
-    multiply(0, lambda k: a0.at[k], lambda k: b0.at[k, xl])
-    multiply(1, lambda k: a1.at[k, xh], lambda k: b1.at[k])
+    keep_rows(y_at[2], 1, xl)
+    keep_cols(z_at[2], 1, xh)
     landed(take.at[0], last_sem.at[0])
     landed(take.at[1], last_sem.at[1])
     out_ref[...] = (
-        total[0] + total[1] + take[0].astype(jnp.float32) + take[1].astype(jnp.float32)
+        total[0, xl] + total[1, xh] + take[0].astype(jnp.float32) + take[1].astype(jnp.float32)
     ).astype(jnp.bfloat16)
 
-    assert len(copies.started) <= 62
     copies.finish()
 
     @pl.when(core == 0)
     def _():
-        pltpu.make_async_copy(a_ref, a0.at[z], send_sem.at[62]).wait()
+        pltpu.make_async_copy(a_ref, a0.at[z], own_sem).wait()
 
     @pl.when(core == 1)
     def _():
-        pltpu.make_async_copy(a_ref.at[own0], a1_own, send_sem.at[62]).wait()
-
-
-def a_rows_at(a1, k, index, core, half):
-    return a1.at[k, index, pl.ds(pl.multiple_of(core * half, half), half)]
+        pltpu.make_async_copy(a_ref.at[own0], a1_own, own_sem).wait()
 
 
 def screen(a, b, panel, near, panel_mask, near_mask, green):
@@ -393,19 +433,20 @@
             pltpu.VMEM((4, 2, depth, cols), bf16),
             pltpu.VMEM((4, depth, cols), bf16),
             pltpu.VMEM((rows // 2, depth), bf16),
-            pltpu.VMEM((2, rows, cols), jnp.float32),
+            pltpu.VMEM((2, 2, rows, cols), jnp.float32),
             pltpu.VMEM((2, rows, cols), bf16),
             pltpu.VMEM((2, rows, cols), bf16),
             pltpu.VMEM((2, 128, 16, NL), bf16),
             pltpu.VMEM((2, 128 * 16, 128), jnp.float32),
             pltpu.VMEM((2, 8, 16 * 32, 128), bf16),
             pltpu.VMEM((2, 16 * 32, 128), bf16),
-            dma((64,)),
+            dma((88,)),
+            dma,
             dma((3,)),
-            dma((4,)),
+            dma((2, 2, 2)),
             dma((6, 2, 2)),
-            dma((6, 2)),
-            dma((3, 4)),
+            dma((6, 2, 2)),
+            dma((3, 4, 2)),
             dma((2,)),
             dma((4,)),
         ],

time: 226 us -> 207 us (0.916)
  Pallas kernels: 215 us -> 197 us
    pallas_call x1, Pallas kernels: 142 us -> 123 us  [screen(): pl.pallas_call(screen_kernel, out_shape=(jax.ShapeDtypeStruct((rows, cols...]
where the time goes in v3:
time: 207 us
  Pallas kernels  197 us (95%)
  local copies, waits for them, and re-layouts  7.22 us (3%)
    pallas_call x1, Pallas kernels, screen(): pl.pallas_call(screen_kernel, out_shape=(jax.ShapeDtypeStruct((rows, cols...  123 us
    pallas_call x1, Pallas kernels, contract(): pl.pallas_call(contract_kernel, out_shape=(jax.ShapeDtypeStruct((rows, co...  74.6 us

profile of v3, /device:TPU:1, one launch (start us, length us, event | category | flops | bytes accessed | tf_op | source)
XLA Modules:
  0.0 206.6 jit_solution(9268192692890292658)
XLA Ops:
  0.6 0.0 copy-start
  0.7 0.8 dynamic-slice_convert_fusion.1
  1.4 0.8 dynamic-slice_convert_fusion
  2.2 0.1 broadcast_in_dim.14
  2.3 0.1 convert_element_type.18
  2.4 0.0 copy-done
  2.4 0.6 constant_dynamic-slice_fusion.1.green
  3.0 0.1 broadcast_in_dim.12
  3.1 0.1 convert_element_type.15
  3.2 0.8 copy.14.near_mask
  4.1 1.0 copy.13.panel_mask
  5.1 122.6 %screen.1 = (bf16[512,256]{1,0:T(8,128)(2,1)}, bf16[8,2048,512]{2,1,0:T(8,128)(2,1)}, bf16[2048,256]{1,0:T(8,128)(2,1)}) custom-call(bf16[512,1664]{1,0:T(8,128)(2,1)} %a_ref.1, bf16[3328,256]{1,0:T(8,128)(2,1)} %b_ref.1, bf16[512,64,256]{2,1,0:T(8,128)(2,1)} %panel.1, bf16[256,64,256]{2,1,0:T(8,128)(2,1)} %near.1, f32[512,256]{1,0:T(8,128)} %copy.13.panel_mask, ...), custom_call_target="tpu_custom_call" | custom-call | tf_op jit(solution)/shard_map/screen/pallas_call | solution.py:421
  127.6 0.0 copy-start.1
  127.6 74.6 %contract.1 = (bf16[2048,256]{1,0:T(8,128)(2,1)}, f32[8,128]{1,0:T(8,128)}) custom-call(bf16[512,256]{1,0:T(8,128)(2,1)} %get-tuple-element.22.s_ref, bf16[8,2048,512]{2,1,0:T(8,128)(2,1)} %get-tuple-element.9.panel_t, bf16[2048,256]{1,0:T(8,128)(2,1)} %get-tuple-element.10.dressed), custom_call_target="tpu_custom_call" | custom-call | tf_op jit(solution)/shard_map/contract/pallas_call | solution.py:655
  202.3 0.8 constant_dynamic-slice_fusion
  203.0 0.7 copy.15
  203.7 0.0 copy-done.1
  203.7 0.7 copy.18
  204.4 2.3 %copy.19 = bf16[256,64,32]{0,2,1:T(8,128)(2,1)} copy(bf16[256,64,32]{0,2,1:T(8,128)(2,1)} %bitcast.10) | data formatting | bytes 2097152
  (2 shorter events, 0.1 us)
Async XLA Ops:
  0.6 1.7 copy-start
  127.6 76.1 %copy-start.1 = (bf16[512,256]{1,0:T(8,128)(2,1)S(1)}, bf16[512,256]{1,0:T(8,128)(2,1)}, u32[]{:S(2)}) copy-start(bf16[512,256]{1,0:T(8,128)(2,1)} %get-tuple-element.22.s_ref) | copy-start | bytes 786436

commit v4 on v3

--- a/solution.py
+++ b/solution.py
@@ -12,10 +12,6 @@
 RB = 64
 AB = 32
 MESH = pl.DeviceIdType.MESH
-
-
-def expand_mask(mask, rows, cols):
-    return jnp.repeat(jnp.repeat(mask, rows, axis=0), cols, axis=1)
 
 
 def place():
@@ -44,7 +40,7 @@
         copy.start()
         self.started.append((copy, None))
 
-    def send_or_keep(self, keep, src, dst, recv_sem, target):
+    def send_if(self, wanted, src, dst, recv_sem, target):
         index = len(self.started)
         copy = pltpu.make_async_remote_copy(
             src_ref=src,
@@ -54,23 +50,15 @@
             device_id=target,
             device_id_type=MESH,
         )
-
-        @pl.when(jnp.logical_not(keep))
-        def _():
-            copy.start()
-
-        @pl.when(keep)
-        def _():
-            pltpu.make_async_copy(src, dst, recv_sem).start()
-
-        self.started.append((copy, keep))
+        pl.when(wanted)(copy.start)
+        self.started.append((copy, wanted))
 
     def finish(self):
-        for copy, keep in self.started:
-            if keep is None:
+        for copy, wanted in self.started:
+            if wanted is None:
                 copy.wait_send()
             else:
-                pl.when(jnp.logical_not(keep))(copy.wait_send)
+                pl.when(wanted)(copy.wait_send)
 
 
 def landed(ref, sem):
@@ -148,9 +136,9 @@
     b_ref,
     panel,
     near,
-    panel_mask,
-    near_mask,
-    green,
+    panel_mask_ref,
+    near_mask_ref,
+    green_ref,
     out_ref,
     panel_t,
     dressed,
@@ -166,6 +154,11 @@
     flat,
     made,
     made_near,
+    panel_blocks,
+    near_blocks,
+    panel_mask,
+    near_mask,
+    green,
     send_sem,
     own_sem,
     local_sem,
@@ -175,7 +168,35 @@
     twin_sem,
     last_sem,
     step_sem,
+    small_sem,
 ):
+    row, col = lax.axis_index("row"), lax.axis_index("col")
+    small = [
+        pltpu.make_async_copy(panel_mask_ref, panel_blocks, small_sem.at[0]),
+        pltpu.make_async_copy(near_mask_ref, near_blocks, small_sem.at[1]),
+        pltpu.make_async_copy(
+            green_ref.at[pl.ds(pl.multiple_of(row * 32, 32), 32)], green, small_sem.at[2]
+        ),
+    ]
+    for copy in small:
+        copy.start()
+
+    def finish_masks():
+        for copy in small:
+            copy.wait()
+        for blocks, mask, begin in (
+            (panel_blocks, panel_mask, row * (panel_mask.shape[0] // RB)),
+            (near_blocks, near_mask, col * (near_mask.shape[0] // RB)),
+        ):
+            count = mask.shape[0]
+            shape = (count, blocks.shape[0])
+            at = lax.broadcasted_iota(jnp.int32, shape, 0) // RB + begin
+            pick = (at == lax.broadcasted_iota(jnp.int32, shape, 1)).astype(jnp.float32)
+            shape = (blocks.shape[1], NL)
+            wide = lax.broadcasted_iota(jnp.int32, shape, 1) // AB == lax.broadcasted_iota(jnp.int32, shape, 0)
+            picked = jnp.dot(pick, blocks[...].astype(jnp.float32), preferred_element_type=jnp.float32)
+            mask[...] = jnp.dot(picked, wide.astype(jnp.float32), preferred_element_type=jnp.float32)
+
     panel_steps, near_steps = prepare(
         panel, near, panel_mask, near_mask, green, panel_t, dressed, taken, flat, made, made_near, step_sem
     )
@@ -244,24 +265,44 @@
     def b_own(p, base=0):
         return b_ref.at[pl.ds(base + p * deep[0], deep[p])]
 
+    inner = xh != xl
+
     def b_along_x(p):
+        def at(role):
+            return b0.at[y, role, pl.ds(p * deep[0], deep[p])]
+
         for j in range(2):
-            keep = jnp.logical_and(j == xh, xh == xl)
-            at = b0.at[y, xl, pl.ds(p * deep[0], deep[p])]
-            copies.send_or_keep(keep, b_own(p), at, x_sem.at[1, xl, p], device(y, j, z, xh, core))
+            copies.send_if(inner, b_own(p), at(0), x_sem.at[1, 0, p], device(y, j, z, xh, core))
 
     def a_along_x(p):
+        source = a1_own.at[pl.ds(p * piece, piece)]
         for j in range(2):
-            keep = jnp.logical_and(j == xl, xh == xl)
-            at = a1.at[z, xh, pl.ds(pl.multiple_of(core * half + p * piece, piece), piece)]
+            copies.send_if(inner, source, a_slot(1, z, p), x_sem.at[0, 0, p], device(y, xl, z, j, core))
+
+    outer = jnp.logical_not(inner)
+
+    def a_outer_along_x(p):
+        source = a1_own.at[pl.ds(p * piece, piece)]
+        copies.send_if(outer, source, a_slot(2, z, p), x_sem.at[0, 1, p], device(y, xh, z, 1 - xl, core))
+
+    def b_outer_along_x(p):
+        copies.send_if(outer, b_own(p), b_slot(2, y, p), x_sem.at[1, 1, p], device(y, 1 - xh, z, xl, core))
+
+    def outer_keep():
+        for p in range(2):
             source = a1_own.at[pl.ds(p * piece, piece)]
-            copies.send_or_keep(keep, source, at, x_sem.at[0, xh, p], device(y, xl, z, j, core))
+            pltpu.make_async_copy(source, a_slot(2, z, p), x_sem.at[0, 1, p]).start()
+            pltpu.make_async_copy(b_own(p), b_slot(2, y, p), x_sem.at[1, 1, p]).start()
 
     def spread(array, stream, p, source=None):
         slot, base, at, to = array
         for side in range(2):
             here = slot(stream, at[0], p)
             copies.send(here if source is None else source, here, near_sem.at[base + stream, side, p], to[side])
+
+    def start_near(wanted, p, source):
+        for side in range(2):
+            copies.send_if(wanted, source, a_slot(0, z, p), near_sem.at[0, side, p], a_up[side])
 
     def to_twin(stream, k, p, index):
         here = a_slot(stream, k, p)
@@ -289,13 +330,12 @@
         for d in indices:
             landed(a_slot(stream, z_at[d], p, of=1 - core), twin_sem.at[stream, d, p])
 
-    def arrive(p):
-        for s in (1, 2):
-            landed(a_slot(s, z, p), x_sem.at[0, s - 1, p])
-            spread(A, s, p)
-            to_twin(s, z, p, 0)
-            landed(b_slot(s, y, p), x_sem.at[1, s - 1, p])
-            spread(B, s, p)
+    def arrive(s, p):
+        landed(a_slot(s, z, p), x_sem.at[0, s - 1, p])
+        spread(A, s, p)
+        landed(b_slot(s, y, p), x_sem.at[1, s - 1, p])
+        spread(B, s, p)
+        to_twin(s, z, p, 0)
 
     def keep_rows(k, p, j):
         lanes = slice(p * deep[0], p * deep[0] + deep[p])
@@ -317,18 +357,9 @@
 
         lax.fori_loop(0, 2, body, 0)
 
-    def multiply(p, distances):
-        def body(j, carry):
-            for d in distances:
-                keep_rows(y_at[d], p, j)
-                keep_cols(z_at[d], p, j)
-            return carry
-
-        lax.fori_loop(0, 2, body, 0)
-
+    for p in range(2):
+        start_near(core == 0, p, a_ref.at[pl.ds(p * piece, piece)])
     b_along_x(0)
-    b_local = pltpu.make_async_copy(b_ref.at[pl.ds(depth, depth)], b1.at[y], local_sem.at[2])
-    b_local.start()
     for p in range(2):
         spread(B, 0, p, b_own(p, depth))
     landed(a1_own, local_sem.at[1])
@@ -337,69 +368,98 @@
     a_along_x(1)
     landed(a0.at[z], local_sem.at[0])
     for p in range(2):
-        spread(A, 0, p)
+        start_near(core == 1, p, a_slot(0, z, p))
+    pl.when(outer)(outer_keep)
+    b_local = pltpu.make_async_copy(b_ref.at[pl.ds(depth, depth)], b1.at[y], local_sem.at[2])
+    b_local.start()
     total[...] = jnp.zeros_like(total)
+    finish_masks()
 
     panel_steps(0, 4)
     go_on(B, 0, 0)
     go_on(A, 0, 0)
-    panel_steps(4, 9)
+    panel_steps(4, 8)
     go_on(B, 0, 1)
     go_on(A, 0, 1)
-    panel_steps(9, 12)
-    arrive(0)
-    panel_steps(12, 16)
+    arrive(1, 0)
+    for p in range(2):
+        a_outer_along_x(p)
+    panel_steps(8, 11)
     for p in range(2):
         far(B, 0, p)
         far(A, 0, p)
-    near_steps(0, 4)
+    arrive(1, 1)
+    for p in range(2):
+        b_outer_along_x(p)
+    panel_steps(11, 14)
     go_on(A, 1, 0)
     go_on(B, 1, 0)
+    panel_steps(14, 16)
+    near_steps(0, 2)
+    arrive(2, 0)
+    go_on(A, 1, 1)
+    go_on(B, 1, 1)
+    near_steps(2, 4)
+    for p in range(2):
+        from_twin(0, p, (1, 2, 3))
+    b_local.wait()
+
+    def others(p):
+        def step(d, carry):
+            keep_rows(lax.rem(y + d, 4), p, 0)
+            keep_cols(lax.rem(z + d, 4), p, 0)
+            return carry
+
+        lax.fori_loop(0, 4, step, 0)
+
+    far(A, 1, 0)
+    far(B, 1, 0)
+    arrive(2, 1)
     near_steps(4, 8)
-    b_local.wait()
+    from_twin(1, 0, (0, 1, 2, 3))
+    others(0)
+    far(A, 1, 1)
+    far(B, 1, 1)
     go_on(A, 2, 0)
     go_on(B, 2, 0)
-    arrive(1)
-    for p in range(2):
-        from_twin(0, p, (1, 2, 3))
-    for s in (1, 2):
-        from_twin(s, 0, (0, 1, 3))
-    multiply(0, (0, 1))
-    for s in (1, 2):
-        far(A, s, 0)
-        far(B, s, 0)
-    multiply(0, (3,))
-    go_on(A, 1, 1)
-    go_on(B, 1, 1)
-    for s in (1, 2):
-        from_twin(s, 0, (2,))
-        from_twin(s, 1, (0,))
-    multiply(0, (2,))
+    from_twin(1, 1, (0, 1, 2, 3))
+    others(1)
+    for i in range(2):
+        give[i] = total[i, 0].astype(jnp.bfloat16)
+    copies.send(give.at[0], take.at[0], last_sem.at[0], device(y, xh, z, 1 - xl, core))
+    copies.send(give.at[1], take.at[1], last_sem.at[1], device(y, 1 - xh, z, xl, core))
+    from_twin(2, 0, (0, 1, 3))
+
+    def own(p):
+        def step(d):
+            keep_rows(y_at[d], p, 1)
+            keep_cols(z_at[d], p, 1)
+
+        return step
+
+    step = own(0)
+    for d in (0, 1, 3):
+        step(d)
     go_on(A, 2, 1)
     go_on(B, 2, 1)
-    multiply(1, (0,))
-    for s in (1, 2):
-        from_twin(s, 1, (1, 3))
-    multiply(1, (1, 3))
-    for s in (1, 2):
-        far(A, s, 1)
-        far(B, s, 1)
-    for s in (1, 2):
-        from_twin(s, 1, (2,))
-
-    keep_rows(y_at[2], 1, 1 - xl)
-    give[0] = total[0, 1 - xl].astype(jnp.bfloat16)
-    copies.send(give.at[0], take.at[0], last_sem.at[0], device(y, xh, z, 1 - xl, core))
-    keep_cols(z_at[2], 1, 1 - xh)
-    give[1] = total[1, 1 - xh].astype(jnp.bfloat16)
-    copies.send(give.at[1], take.at[1], last_sem.at[1], device(y, 1 - xh, z, xl, core))
-    keep_rows(y_at[2], 1, xl)
-    keep_cols(z_at[2], 1, xh)
+    far(A, 2, 0)
+    far(B, 2, 0)
+    from_twin(2, 0, (2,))
+    from_twin(2, 1, (0, 1, 3))
+    step(2)
+    step = own(1)
+    for d in (0, 1, 3):
+        step(d)
+    far(B, 2, 1)
+    keep_rows(y_at[2], 1, 1)
+    far(A, 2, 1)
     landed(take.at[0], last_sem.at[0])
     landed(take.at[1], last_sem.at[1])
-    out_ref[...] = (
-        total[0, xl] + total[1, xh] + take[0].astype(jnp.float32) + take[1].astype(jnp.float32)
-    ).astype(jnp.bfloat16)
+    total[0, 1] += total[1, 1] + take[0].astype(jnp.float32) + take[1].astype(jnp.float32)
+    total[1, 1] = jnp.zeros_like(total[1, 1])
+    from_twin(2, 1, (2,))
+    keep_cols(z_at[2], 1, 1)
+    out_ref[...] = (total[0, 1] + total[1, 1]).astype(jnp.bfloat16)
 
     copies.finish()
 
@@ -425,7 +485,7 @@
             jax.ShapeDtypeStruct((8, TILE * 32, rows), bf16),
             jax.ShapeDtypeStruct((TILE * 32, cols), bf16),
         ),
-        in_specs=[hbm] * 4 + [vmem] * 3,
+        in_specs=[hbm] * 7,
         out_specs=(vmem, hbm, hbm),
         scratch_shapes=[
             pltpu.VMEM((4, rows, depth), bf16),
@@ -440,7 +500,12 @@
             pltpu.VMEM((2, 128 * 16, 128), jnp.float32),
             pltpu.VMEM((2, 8, 16 * 32, 128), bf16),
             pltpu.VMEM((2, 16 * 32, 128), bf16),
-            dma((88,)),
+            pltpu.VMEM(panel_mask.shape, jnp.int32),
+            pltpu.VMEM(near_mask.shape, jnp.int32),
+            pltpu.VMEM((rows, NL), jnp.float32),
+            pltpu.VMEM((cols, NL), jnp.float32),
+            pltpu.VMEM((32, NL), bf16),
+            dma((96,)),
             dma,
             dma((3,)),
             dma((2, 2, 2)),
@@ -449,6 +514,7 @@
             dma((3, 4, 2)),
             dma((2,)),
             dma((4,)),
+            dma((3,)),
         ],
         compiler_params=pltpu.CompilerParams(
             collective_id=0, has_side_effects=True, vmem_limit_bytes=56 * 2**20
@@ -607,23 +673,29 @@
         for h in range(2):
             total[h, at] = result[:, h * 128 : (h + 1) * 128].astype(f32)
 
+    def column(ref, l, start, count):
+        halves = [ref[h, pl.ds(start * 32 + l, count, stride=32), :].astype(bf16) for h in range(2)]
+        return jnp.concatenate(halves, 1)
+
+    def energy(start):
+        result = jnp.zeros((TILE // 2, TILE), f32)
+        for l in range(32):
+            result = result + lax.dot_general(
+                column(total, l, start, TILE // 2),
+                column(other, l, 0, TILE),
+                (((1,), (1,)), ((), ())),
+                preferred_element_type=f32,
+            )
+        tile[start : start + TILE // 2] = jnp.concatenate([-result, jnp.zeros_like(result)], 1)
+
     both_near(0, near_y.at[0])
     landed(cross_x.at[0], cross_sem.at[0])
     landed(cross_y, cross_sem.at[4])
     settle(pl.ds(0, LATE), late(0, 0), near_y.at[0, 0], near_y.at[0, 1], cross_y)
+    energy(0)
     both_near(2, near_x)
     settle(pl.ds(LATE, early), first(0, 0), cross_x.at[0], near_x.at[0], near_x.at[1])
-
-    def column(ref, l):
-        halves = [ref[h, pl.ds(l, TILE, stride=32), :].astype(bf16) for h in range(2)]
-        return jnp.concatenate(halves, 1)
-
-    energy = jnp.zeros((TILE, TILE), f32)
-    for l in range(32):
-        energy = energy + lax.dot_general(
-            column(total, l), column(other, l), (((1,), (1,)), ((), ())), preferred_element_type=f32
-        )
-    tile[...] = jnp.concatenate([-energy, jnp.zeros_like(energy)], 1)
+    energy(TILE // 2)
 
     def share_of(row):
         return pl.ds(pl.multiple_of(row * 8, 8), 8)
@@ -691,25 +763,12 @@
 def per_device(
     polarization, metric, three_panel, three_near, green_function, mask_panel, mask_near
 ):
-    row_index = lax.axis_index("row")
+    row_count = lax.axis_size("row")
     col_index = lax.axis_index("col")
-    row_count = lax.axis_size("row")
-    panel_rows = polarization.shape[0]
     near_cols = metric.shape[1]
-    panel_blocks = panel_rows // RB
-    panel_mask = lax.dynamic_slice_in_dim(mask_panel, row_index * panel_blocks, panel_blocks, 0)
-    near_blocks = near_cols // RB
-    near_mask = lax.dynamic_slice_in_dim(mask_near, col_index * near_blocks, near_blocks, 0)
     near_share = NL // row_count
-    green = lax.dynamic_slice_in_dim(green_function, row_index * near_share, near_share, 0)
     screened, panel_t, dressed = screen(
-        polarization,
-        metric,
-        three_panel,
-        three_near,
-        expand_mask(panel_mask, RB, AB).astype(jnp.float32),
-        expand_mask(near_mask, RB, AB).astype(jnp.float32),
-        green,
+        polarization, metric, three_panel, three_near, mask_panel, mask_near, green_function
     )
     contracted, energy = contract(screened, panel_t, dressed)
     contracted = contracted.T.reshape(near_cols, TILE, near_share)

time: 207 us -> 188 us (0.908)
  Pallas kernels: 197 us -> 179 us
    pallas_call x1, Pallas kernels: 123 us -> 101 us  [screen(): pl.pallas_call(screen_kernel, out_shape=(jax.ShapeDtypeStruct((rows, cols...]
    pallas_call x1, Pallas kernels: 74.6 us -> 78 us  [contract(): pl.pallas_call(contract_kernel, out_shape=(jax.ShapeDtypeStruct((rows, co...]
    unnamed x7, local copies, waits for them, and re-layouts: 3.63 us -> 6.39 us
where the time goes in v4:
time: 188 us; the launch traced here: 187 us
  Pallas kernels  179 us (95%)
  local copies, waits for them, and re-layouts  7.15 us (4%)
    pallas_call x1, Pallas kernels, screen(): pl.pallas_call(screen_kernel, out_shape=(jax.ShapeDtypeStruct((rows, cols...  101 us
    pallas_call x1, Pallas kernels, contract(): pl.pallas_call(contract_kernel, out_shape=(jax.ShapeDtypeStruct((rows, co...  78 us
    unnamed x7, local copies, waits for them, and re-layouts  6.39 us

profile of v4, /device:TPU:1, one launch (start us, length us, event | category | flops | bytes accessed | tf_op | source)
XLA Modules:
  0.0 186.9 jit_solution(3142730016373284587)
XLA Ops:
  0.6 1.4 copy.10.panel_mask_ref
  2.0 1.4 copy.11.near_mask_ref
  3.4 101.1 %screen.1 = (bf16[512,256]{1,0:T(8,128)(2,1)}, bf16[8,2048,512]{2,1,0:T(8,128)(2,1)}, bf16[2048,256]{1,0:T(8,128)(2,1)}) custom-call(bf16[512,1664]{1,0:T(8,128)(2,1)} %a_ref.1, bf16[3328,256]{1,0:T(8,128)(2,1)} %b_ref.1, bf16[512,64,256]{2,1,0:T(8,128)(2,1)} %panel.1, bf16[256,64,256]{2,1,0:T(8,128)(2,1)} %near.1, s32[64,8]{1,0:T(8,128)} %copy.10.panel_mask_ref, ...), custom_call_target="tpu_custom_call" | custom-call | tf_op jit(solution)/shard_map/screen/pallas_call | solution.py:481
  104.5 0.0 copy-start
  104.5 78.0 %contract.1 = (bf16[2048,256]{1,0:T(8,128)(2,1)}, f32[8,128]{1,0:T(8,128)}) custom-call(bf16[512,256]{1,0:T(8,128)(2,1)} %get-tuple-element.19.s_ref, bf16[8,2048,512]{2,1,0:T(8,128)(2,1)} %get-tuple-element.9.panel_t, bf16[2048,256]{1,0:T(8,128)(2,1)} %get-tuple-element.10.dressed), custom_call_target="tpu_custom_call" | custom-call | tf_op jit(solution)/shard_map/contract/pallas_call | solution.py:727
  182.5 0.8 constant_dynamic-slice_fusion
  183.3 0.7 copy.12
  183.9 0.0 copy-done
  183.9 0.7 copy.15
  184.6 2.3 %copy.16 = bf16[256,64,32]{0,2,1:T(8,128)(2,1)} copy(bf16[256,64,32]{0,2,1:T(8,128)(2,1)} %bitcast.3) | data formatting | bytes 2097152
Async XLA Ops:
  104.5 79.4 %copy-start = (bf16[512,256]{1,0:T(8,128)(2,1)S(1)}, bf16[512,256]{1,0:T(8,128)(2,1)}, u32[]{:S(2)}) copy-start(bf16[512,256]{1,0:T(8,128)(2,1)} %get-tuple-element.19.s_ref) | copy-start | bytes 786436

commit v5 on v4

--- a/solution.py
+++ b/solution.py
@@ -131,7 +131,7 @@
     )
 
 
-def screen_kernel(
+def screen_part(
     a_ref,
     b_ref,
     panel,
@@ -142,6 +142,7 @@
     out_ref,
     panel_t,
     dressed,
+    ahead,
     a0,
     a1,
     b0,
@@ -189,12 +190,14 @@
             (near_blocks, near_mask, col * (near_mask.shape[0] // RB)),
         ):
             count = mask.shape[0]
-            shape = (count, blocks.shape[0])
+            shape = (count, blocks.shape[1])
             at = lax.broadcasted_iota(jnp.int32, shape, 0) // RB + begin
             pick = (at == lax.broadcasted_iota(jnp.int32, shape, 1)).astype(jnp.float32)
-            shape = (blocks.shape[1], NL)
+            shape = (blocks.shape[0], NL)
             wide = lax.broadcasted_iota(jnp.int32, shape, 1) // AB == lax.broadcasted_iota(jnp.int32, shape, 0)
-            picked = jnp.dot(pick, blocks[...].astype(jnp.float32), preferred_element_type=jnp.float32)
+            picked = lax.dot_general(
+                pick, blocks[...].astype(jnp.float32), (((1,), (1,)), ((), ())), preferred_element_type=jnp.float32
+            )
             mask[...] = jnp.dot(picked, wide.astype(jnp.float32), preferred_element_type=jnp.float32)
 
     panel_steps, near_steps = prepare(
@@ -202,19 +205,15 @@
     )
     y, xh, z, xl, core = place()
     twin = device(y, xh, z, xl, 1 - core)
-    x = xh * 2 + xl
     rows, depth = a_ref.shape
     half, piece = rows // 2, rows // 4
     z_at = [lax.rem(z + d, 4) for d in range(4)]
     y_at = [lax.rem(y + d, 4) for d in range(4)]
 
     barrier = pltpu.get_barrier_semaphore()
-    partners = [twin]
-    partners += [device(y, xh, z_at[d], xl, core) for d in (1, 3)]
-    partners += [device(y_at[d], xh, z, xl, core) for d in (1, 3)]
-    for d in (1, 2, 3):
-        other = lax.rem(x + d, 4)
-        partners.append(device(y, other // 2, z, other % 2, core))
+    partners = [device(lax.rem(y + k // 2, 4), lax.rem(xh + k, 2), z, xl, core) for k in range(1, 8)]
+    partners += [(row, lax.rem(col + k, 16)) for k in range(1, 16)]
+    partners.append(device(y, 1 - xh, z, 1 - xl, core))
     for partner in partners:
         pl.semaphore_signal(barrier, inc=1, device_id=partner, device_id_type=MESH)
     pl.semaphore_wait(barrier, len(partners))
@@ -450,6 +449,7 @@
     step = own(1)
     for d in (0, 1, 3):
         step(d)
+    ahead()
     far(B, 2, 1)
     keep_rows(y_at[2], 1, 1)
     far(A, 2, 1)
@@ -461,72 +461,24 @@
     keep_cols(z_at[2], 1, 1)
     out_ref[...] = (total[0, 1] + total[1, 1]).astype(jnp.bfloat16)
 
-    copies.finish()
-
-    @pl.when(core == 0)
-    def _():
-        pltpu.make_async_copy(a_ref, a0.at[z], own_sem).wait()
-
-    @pl.when(core == 1)
-    def _():
-        pltpu.make_async_copy(a_ref.at[own0], a1_own, own_sem).wait()
-
-
-def screen(a, b, panel, near, panel_mask, near_mask, green):
-    rows, depth = a.shape
-    cols = b.shape[1]
-    bf16 = jnp.bfloat16
-    dma = pltpu.SemaphoreType.DMA
-    hbm, vmem = pl.BlockSpec(memory_space=pl.ANY), pl.BlockSpec(memory_space=pltpu.VMEM)
-    return pl.pallas_call(
-        screen_kernel,
-        out_shape=(
-            jax.ShapeDtypeStruct((rows, cols), bf16),
-            jax.ShapeDtypeStruct((8, TILE * 32, rows), bf16),
-            jax.ShapeDtypeStruct((TILE * 32, cols), bf16),
-        ),
-        in_specs=[hbm] * 7,
-        out_specs=(vmem, hbm, hbm),
-        scratch_shapes=[
-            pltpu.VMEM((4, rows, depth), bf16),
-            pltpu.VMEM((4, 2, rows, depth), bf16),
-            pltpu.VMEM((4, 2, depth, cols), bf16),
-            pltpu.VMEM((4, depth, cols), bf16),
-            pltpu.VMEM((rows // 2, depth), bf16),
-            pltpu.VMEM((2, 2, rows, cols), jnp.float32),
-            pltpu.VMEM((2, rows, cols), bf16),
-            pltpu.VMEM((2, rows, cols), bf16),
-            pltpu.VMEM((2, 128, 16, NL), bf16),
-            pltpu.VMEM((2, 128 * 16, 128), jnp.float32),
-            pltpu.VMEM((2, 8, 16 * 32, 128), bf16),
-            pltpu.VMEM((2, 16 * 32, 128), bf16),
-            pltpu.VMEM(panel_mask.shape, jnp.int32),
-            pltpu.VMEM(near_mask.shape, jnp.int32),
-            pltpu.VMEM((rows, NL), jnp.float32),
-            pltpu.VMEM((cols, NL), jnp.float32),
-            pltpu.VMEM((32, NL), bf16),
-            dma((96,)),
-            dma,
-            dma((3,)),
-            dma((2, 2, 2)),
-            dma((6, 2, 2)),
-            dma((6, 2, 2)),
-            dma((3, 4, 2)),
-            dma((2,)),
-            dma((4,)),
-            dma((3,)),
-        ],
-        compiler_params=pltpu.CompilerParams(
-            collective_id=0, has_side_effects=True, vmem_limit_bytes=56 * 2**20
-        ),
-        name="screen",
-    )(a, b, panel, near, panel_mask, near_mask, green)
+    def finish():
+        copies.finish()
+
+        @pl.when(core == 0)
+        def _():
+            pltpu.make_async_copy(a_ref, a0.at[z], own_sem).wait()
+
+        @pl.when(core == 1)
+        def _():
+            pltpu.make_async_copy(a_ref.at[own0], a1_own, own_sem).wait()
+
+    return finish
 
 
 LATE = 1152
 
 
-def contract_kernel(
+def contract_part(
     s_ref,
     panel_t,
     dressed,
@@ -542,7 +494,6 @@
     near_x,
     total,
     other,
-    dressed_b,
     tile,
     row_sum,
     tile_row,
@@ -565,22 +516,21 @@
     def in_col(d):
         return (y * 2 + xh, lax.rem(col + d, 16))
 
-    partners = [in_row(s // 2, s % 2) for s in range(1, 8)] + [in_col(d) for d in range(1, 16)]
-    barrier = pltpu.get_barrier_semaphore()
-    for partner in partners:
-        pl.semaphore_signal(barrier, inc=1, device_id=partner, device_id_type=MESH)
-
     order = [(2, 1), (2, 0), (1, 1), (3, 1), (1, 0), (3, 0), (0, 1), (0, 0)]
+    chunk = block.shape[1]
 
     def fetch(i):
-        d, j = order[i]
+        d, j = order[i // 2]
         share = lax.rem(y + d, 4) * 2 + lax.rem(xh + j, 2)
-        return pltpu.make_async_copy(panel_t.at[share], block.at[i % 2], block_sem.at[i % 2])
+        return pltpu.make_async_copy(
+            panel_t.at[share, pl.ds(i % 2 * chunk, chunk)], block.at[i % 2], block_sem.at[i % 2]
+        )
 
     fetch(0).start()
-    dressed_copy = pltpu.make_async_copy(dressed, dressed_b, block_sem.at[2])
-    dressed_copy.start()
-    pl.semaphore_wait(barrier, len(partners))
+    fetch(1).start()
+    for h in range(2):
+        other[h] = dressed[:, h * 128 : (h + 1) * 128].astype(f32)
+    yield
 
     copies = Copies(send_sem)
     rows = TILE * 32
@@ -595,18 +545,20 @@
         return part.at[d * 2 + j, pl.ds(LATE + start, count)]
 
     for i, (d, j) in enumerate(order):
-        if i + 1 < 8:
-            fetch(i + 1).start()
-        fetch(i).wait()
-
-        def multiply(t, carry):
-            at = pl.ds(pl.multiple_of(t * 256, 256), 256)
-            part[d * 2 + j, at] = jnp.dot(
-                block[i % 2, at], s_ref[...], preferred_element_type=f32
-            ).astype(bf16)
-            return carry
-
-        lax.fori_loop(0, rows // 256, multiply, 0)
+        for h in range(2):
+            fetch(i * 2 + h).wait()
+
+            def multiply(t, carry):
+                at = pl.ds(pl.multiple_of(t * 256, 256), 256)
+                to = pl.ds(pl.multiple_of(h * chunk + t * 256, 256), 256)
+                part[d * 2 + j, to] = jnp.dot(
+                    block[h, at], s_ref[...], preferred_element_type=f32
+                ).astype(bf16)
+                return carry
+
+            lax.fori_loop(0, chunk // 256, multiply, 0)
+            if i < 7:
+                fetch(i * 2 + 2 + h).start()
         if j == 1:
             copies.send(first(d, 1), cross_x.at[d], cross_sem.at[d], across)
         if d == 2:
@@ -659,10 +611,6 @@
     landed(far_x.at[1], far_sem.at[2, 1])
     add(first(3, 0, h_early, h_early), far_x.at[1])
     copies.send(first(3, 0, h_early, h_early), near_x.at[1, pl.ds(h_early, h_early)], near_sem.at[2, 1, 1], down)
-
-    dressed_copy.wait()
-    for h in range(2):
-        other[h] = dressed_b[:, h * 128 : (h + 1) * 128].astype(f32)
 
     def settle(at, *terms):
         result = terms[0][...].astype(f32)
@@ -713,67 +661,132 @@
     for d in range(1, 16):
         landed(tile_col.at[d], col_sem.at[d])
         mine = mine + tile_col[d]
-    energy_ref[...] = mine
+    turned = pltpu.roll(mine, lax.rem(128 - 4 * col, 128), 1).T
+    energy_ref[...] = turned[:4]
     copies.finish()
 
 
-def contract(screened, panel_t, dressed):
-    rows = TILE * 32
-    cols = screened.shape[1]
-    early = rows - LATE
+SCREEN_SCRATCH = 27
+
+
+def kernel(*refs):
+    inputs, (screened, contracted, energy, panel_t), scratch = refs[:7], refs[7:11], refs[11:]
+    dressed, (first, second) = scratch[0], (scratch[1 : 1 + SCREEN_SCRATCH], scratch[1 + SCREEN_SCRATCH :])
+    flat = first[9]
+    steps = contract_part(screened, panel_t, dressed, contracted, energy, *second[:8], flat, *second[8:])
+    finish = screen_part(*inputs, screened, panel_t, dressed, lambda: next(steps), *first)
+    next(steps, None)
+    finish()
+
+
+def tile_terms(a, b, panel, near, panel_mask, near_mask, green):
+    rows, depth = a.shape
+    cols = b.shape[1]
+    long = TILE * 32
+    early = long - LATE
     bf16, f32 = jnp.bfloat16, jnp.float32
     dma = pltpu.SemaphoreType.DMA
     hbm, vmem = pl.BlockSpec(memory_space=pl.ANY), pl.BlockSpec(memory_space=pltpu.VMEM)
+    first = [
+        pltpu.VMEM((4, rows, depth), bf16),
+        pltpu.VMEM((4, 2, rows, depth), bf16),
+        pltpu.VMEM((4, 2, depth, cols), bf16),
+        pltpu.VMEM((4, depth, cols), bf16),
+        pltpu.VMEM((rows // 2, depth), bf16),
+        pltpu.VMEM((2, 2, rows, cols), f32),
+        pltpu.VMEM((2, rows, cols), bf16),
+        pltpu.VMEM((2, rows, cols), bf16),
+        pltpu.VMEM((2, 128, 16, NL), bf16),
+        pltpu.VMEM((2, 128 * 16, 128), f32),
+        pltpu.VMEM((2, 8, 16 * 32, 128), bf16),
+        pltpu.VMEM((2, 16 * 32, 128), bf16),
+        pltpu.VMEM(panel_mask.shape, jnp.int32),
+        pltpu.VMEM(near_mask.shape, jnp.int32),
+        pltpu.VMEM((rows, NL), f32),
+        pltpu.VMEM((cols, NL), f32),
+        pltpu.VMEM((32, NL), bf16),
+        dma((96,)),
+        dma,
+        dma((3,)),
+        dma((2, 2, 2)),
+        dma((6, 2, 2)),
+        dma((6, 2, 2)),
+        dma((3, 4, 2)),
+        dma((2,)),
+        dma((4,)),
+        dma((3,)),
+    ]
+    second = [
+        pltpu.VMEM((2, long // 2, rows), bf16),
+        pltpu.VMEM((8, long, cols), bf16),
+        pltpu.VMEM((2, 2, LATE // 2, cols), bf16),
+        pltpu.VMEM((2, 2, LATE, cols), bf16),
+        pltpu.VMEM((LATE, cols), bf16),
+        pltpu.VMEM((4, early, cols), bf16),
+        pltpu.VMEM((2, early // 2, cols), bf16),
+        pltpu.VMEM((2, early, cols), bf16),
+        pltpu.VMEM((2, long, 128), f32),
+        pltpu.VMEM((TILE, 128), f32),
+        pltpu.VMEM((8, 128), f32),
+        pltpu.VMEM((8, 8, 128), f32),
+        pltpu.VMEM((16, 8, 128), f32),
+        dma((48,)),
+        dma((2,)),
+        dma((3, 2)),
+        dma((3, 2, 2)),
+        dma((5,)),
+        dma((8,)),
+        dma((16,)),
+    ]
+    assert len(first) == SCREEN_SCRATCH
     return pl.pallas_call(
-        contract_kernel,
-        out_shape=(jax.ShapeDtypeStruct((rows, cols), bf16), jax.ShapeDtypeStruct((8, 128), f32)),
-        in_specs=[vmem, hbm, hbm],
-        out_specs=(vmem, vmem),
-        scratch_shapes=[
-            pltpu.VMEM((2, rows, screened.shape[0]), bf16),
-            pltpu.VMEM((8, rows, cols), bf16),
-            pltpu.VMEM((2, 2, LATE // 2, cols), bf16),
-            pltpu.VMEM((2, 2, LATE, cols), bf16),
-            pltpu.VMEM((LATE, cols), bf16),
-            pltpu.VMEM((4, early, cols), bf16),
-            pltpu.VMEM((2, early // 2, cols), bf16),
-            pltpu.VMEM((2, early, cols), bf16),
-            pltpu.VMEM((2, rows, 128), f32),
-            pltpu.VMEM((2, rows, 128), f32),
-            pltpu.VMEM((rows, cols), bf16),
-            pltpu.VMEM((TILE, 128), f32),
-            pltpu.VMEM((8, 128), f32),
-            pltpu.VMEM((8, 8, 128), f32),
-            pltpu.VMEM((16, 8, 128), f32),
-            dma((48,)),
-            dma((3,)),
-            dma((3, 2)),
-            dma((3, 2, 2)),
-            dma((5,)),
-            dma((8,)),
-            dma((16,)),
-        ],
+        kernel,
+        out_shape=(
+            jax.ShapeDtypeStruct((rows, cols), bf16),
+            jax.ShapeDtypeStruct((long, cols), bf16),
+            jax.ShapeDtypeStruct((4, 8), f32),
+            jax.ShapeDtypeStruct((8, long, rows), bf16),
+        ),
+        in_specs=[hbm] * 7,
+        out_specs=(vmem, vmem, vmem, hbm),
+        scratch_shapes=[pltpu.VMEM((long, cols), bf16)] + first + second,
         compiler_params=pltpu.CompilerParams(
-            collective_id=1, has_side_effects=True, vmem_limit_bytes=56 * 2**20
+            collective_id=0, has_side_effects=True, vmem_limit_bytes=64 * 2**20 - 2**16
         ),
-        name="contract",
-    )(screened, panel_t, dressed)
+        name="tile_terms",
+    )(a, b, panel, near, panel_mask, near_mask, green)
+
+
+def hand_over_kernel(*refs):
+    sources, results, sem = refs[:3], refs[3:6], refs[6]
+    copies = [pltpu.make_async_copy(sources[i], results[i], sem.at[i]) for i in range(3)]
+    for copy in copies:
+        copy.start()
+    for copy in copies:
+        copy.wait()
+
+
+def hand_over(*arrays):
+    hbm = pl.BlockSpec(memory_space=pl.ANY)
+    return pl.pallas_call(
+        hand_over_kernel,
+        out_shape=tuple(jax.ShapeDtypeStruct(array.shape, array.dtype) for array in arrays),
+        in_specs=[hbm] * 3,
+        out_specs=(hbm,) * 3,
+        scratch_shapes=[pltpu.SemaphoreType.DMA((3,))],
+        name="hand_over",
+    )(*arrays)
 
 
 def per_device(
     polarization, metric, three_panel, three_near, green_function, mask_panel, mask_near
 ):
-    row_count = lax.axis_size("row")
-    col_index = lax.axis_index("col")
     near_cols = metric.shape[1]
-    near_share = NL // row_count
-    screened, panel_t, dressed = screen(
-        polarization, metric, three_panel, three_near, mask_panel, mask_near, green_function
+    screened, contracted, energy, _ = tile_terms(
+        polarization, metric, three_panel, three_near, mask_panel.T, mask_near.T, green_function
     )
-    contracted, energy = contract(screened, panel_t, dressed)
-    contracted = contracted.T.reshape(near_cols, TILE, near_share)
-    self_energy = lax.dynamic_slice_in_dim(energy, col_index * 4, 4, 1)
-    return (screened, contracted, self_energy)
+    screened, contracted, energy = hand_over(screened, contracted, energy)
+    return screened, contracted.T.reshape(near_cols, TILE, contracted.shape[0] // TILE), energy.T
 
 
 def solution(mesh):

time: 188 us -> 218 us (1.16)
  Pallas kernels: 179 us -> 216 us
  local copies, waits for them, and re-layouts: 7.15 us -> 0 us
    pallas_call x2, Pallas kernels: 179 us -> 216 us  [the longest x1 175 us: tile_terms(): pl.pallas_call(kernel, out_shape=(jax.ShapeDtypeStruct((rows, cols), bf16...]
    unnamed x7 -> x0, local copies, waits for them, and re-layouts: 6.39 us -> none
where the time goes in v5:
time: 218 us; the launch traced here: 217 us
  Pallas kernels  216 us (99%)
    pallas_call x1, Pallas kernels, tile_terms(): pl.pallas_call(kernel, out_shape=(jax.ShapeDtypeStruct((rows, cols), bf16...  175 us
    pallas_call x1, Pallas kernels, hand_over(): pl.pallas_call(hand_over_kernel, out_shape=tuple((jax.ShapeDtypeStruct(ar...  40.9 us

profile of v5, /device:TPU:1, one launch (start us, length us, event | category | flops | bytes accessed | tf_op | source)
XLA Modules:
  0.0 216.7 jit_solution(11186617413469578268)
XLA Ops:
  0.6 175.0 %tile_terms.1 = (bf16[512,256]{1,0:T(8,128)(2,1)}, bf16[2048,256]{1,0:T(8,128)(2,1)}, f32[4,8]{1,0:T(4,128)}, bf16[8,2048,512]{2,1,0:T(8,128)(2,1)}) custom-call(bf16[512,1664]{1,0:T(8,128)(2,1)} %refs_0_.1, bf16[3328,256]{1,0:T(8,128)(2,1)} %refs_1_.1, bf16[512,64,256]{2,1,0:T(8,128)(2,1)} %refs_2_.1, bf16[256,64,256]{2,1,0:T(8,128)(2,1)} %refs_3_.1, ...), custom_call_target="tpu_custom_call" | custom-call | tf_op jit(solution)/shard_map/tile_terms/pallas_call | solution.py:742
  175.6 40.9 %hand_over.1 = (bf16[512,256]{1,0:T(8,128)(2,1)}, bf16[2048,256]{1,0:T(8,128)(2,1)}, f32[4,8]{1,0:T(4,128)}) custom-call(bf16[512,256]{1,0:T(8,128)(2,1)} %get-tuple-element.9.refs_0_, bf16[2048,256]{1,0:T(8,128)(2,1)} %get-tuple-element.10.refs_1_, f32[4,8]{1,0:T(4,128)} %get-tuple-element.11.refs_2_), custom_call_target="tpu_custom_call" | custom-call | tf_op jit(solution)/shard_map/hand_over/pallas_call | solution.py:771

commit v6 on v5

--- a/solution.py
+++ b/solution.py
@@ -65,7 +65,7 @@
     pltpu.make_async_copy(ref, ref, sem).wait()
 
 
-def prepare(panel, near, panel_mask, near_mask, green, panel_t, dressed, taken, flat, made, made_near, sem):
+def prepare(panel, near, panel_mask, near_mask, green, panel_t, dressed, taken, flat, made, sem):
     start = lambda k, size: pl.ds(pl.multiple_of(k * size, size), size)
 
     def steps(source, mask, count, make, put, first, last):
@@ -106,13 +106,12 @@
         put(last - 2).wait()
         put(last - 1).wait()
 
-    def put_panel(i):
-        place_at = panel_t.at[:, start(i % 4, 512), start(i // 4, 128)]
-        return pltpu.make_async_copy(made.at[i % 2], place_at, sem.at[2 + i % 2])
-
-    def put_near(i):
-        place_at = dressed.at[start(i % 4, 512), start(i // 4, 128)]
-        return pltpu.make_async_copy(made_near.at[i % 2], place_at, sem.at[2 + i % 2])
+    def put_to(result):
+        def put(i):
+            place_at = result.at[:, start(i % 4, 512), start(i // 4, 128)]
+            return pltpu.make_async_copy(made.at[i % 2], place_at, sem.at[2 + i % 2])
+
+        return put
 
     def make_panel(i, m, halves):
         turned = jnp.concatenate([half.T.astype(jnp.bfloat16) for half in halves], 0)
@@ -123,11 +122,11 @@
         product = lax.dot_general(
             green[...], block, (((1,), (1,)), ((), ())), preferred_element_type=jnp.float32
         )
-        made_near[i % 2, m * 32 : (m + 1) * 32, :] = product.astype(jnp.bfloat16)
+        made[i % 2, :, m * 32 : (m + 1) * 32, :] = product.astype(jnp.bfloat16).reshape(8, 32, 128)
 
     return (
-        functools.partial(steps, panel, panel_mask, 16, make_panel, put_panel),
-        functools.partial(steps, near, near_mask, 8, make_near, put_near),
+        functools.partial(steps, panel, panel_mask, 16, make_panel, put_to(panel_t)),
+        functools.partial(steps, near, near_mask, 8, make_near, put_to(dressed)),
     )
 
 
@@ -154,7 +153,6 @@
     taken,
     flat,
     made,
-    made_near,
     panel_blocks,
     near_blocks,
     panel_mask,
@@ -175,9 +173,7 @@
     small = [
         pltpu.make_async_copy(panel_mask_ref, panel_blocks, small_sem.at[0]),
         pltpu.make_async_copy(near_mask_ref, near_blocks, small_sem.at[1]),
-        pltpu.make_async_copy(
-            green_ref.at[pl.ds(pl.multiple_of(row * 32, 32), 32)], green, small_sem.at[2]
-        ),
+        pltpu.make_async_copy(green_ref, green, small_sem.at[2]),
     ]
     for copy in small:
         copy.start()
@@ -201,7 +197,7 @@
             mask[...] = jnp.dot(picked, wide.astype(jnp.float32), preferred_element_type=jnp.float32)
 
     panel_steps, near_steps = prepare(
-        panel, near, panel_mask, near_mask, green, panel_t, dressed, taken, flat, made, made_near, step_sem
+        panel, near, panel_mask, near_mask, green, panel_t, dressed, taken, flat, made, step_sem
     )
     y, xh, z, xl, core = place()
     twin = device(y, xh, z, xl, 1 - core)
@@ -494,6 +490,7 @@
     near_x,
     total,
     other,
+    dressed_b,
     tile,
     row_sum,
     tile_row,
@@ -528,8 +525,6 @@
 
     fetch(0).start()
     fetch(1).start()
-    for h in range(2):
-        other[h] = dressed[:, h * 128 : (h + 1) * 128].astype(f32)
     yield
 
     copies = Copies(send_sem)
@@ -575,7 +570,44 @@
             result = result + each[...].astype(f32)
         ref[...] = result.astype(bf16)
 
-    for j in (1, 0):
+    def share(d, j):
+        return lax.rem(y + d, 4) * 2 + lax.rem(xh + j, 2)
+
+    turns = [(1, 1), (3, 1), (1, 0), (3, 0), (2, 0), (2, 1), (0, 1), (0, 0)]
+
+    def fetch_dressed(i):
+        return pltpu.make_async_copy(dressed.at[share(*turns[i])], dressed_b, block_sem.at[2])
+
+    fetch_dressed(0).start()
+    tile[...] = jnp.zeros_like(tile)
+
+    def energy(i):
+        d, j = turns[i]
+        fetch_dressed(i).wait()
+        for h in range(2):
+            lanes = slice(h * 128, (h + 1) * 128)
+            other[h] = dressed_b[:, lanes].astype(f32)
+            total[h] = part[d * 2 + j, :, lanes].astype(f32)
+        if i < 7:
+            fetch_dressed(i + 1).start()
+
+        def column(ref, l):
+            halves = [ref[h, pl.ds(l, TILE, stride=32), :].astype(bf16) for h in range(2)]
+            return jnp.concatenate(halves, 1)
+
+        def body(k, carry):
+            for l in range(4):
+                carry = carry + lax.dot_general(
+                    column(total, k * 4 + l),
+                    column(other, k * 4 + l),
+                    (((1,), (1,)), ((), ())),
+                    preferred_element_type=f32,
+                )
+            return carry
+
+        tile[:, :TILE] += lax.fori_loop(0, 8, body, jnp.zeros((TILE, TILE), f32))
+
+    def forward_y(j):
         landed(far_y.at[j, 0], far_sem.at[j, 0])
         add(late(1, j, 0, h_late), far_y.at[j, 0])
         copies.send(late(1, j, 0, h_late), near_y.at[j, 0, pl.ds(0, h_late)], near_sem.at[j, 0, 1], up)
@@ -583,6 +615,29 @@
         add(late(3, j, h_late, h_late), far_y.at[j, 1])
         copies.send(late(3, j, h_late, h_late), near_y.at[j, 1, pl.ds(h_late, h_late)], near_sem.at[j, 1, 1], down)
 
+    def both_near(j, ref):
+        count = ref.shape[1] // 2
+        for side in range(2):
+            for turn in range(2):
+                start = count if (side == 0) == (turn == 0) else 0
+                landed(ref.at[side, pl.ds(start, count)], near_sem.at[j, side, turn])
+
+    def share_of(row):
+        return pl.ds(pl.multiple_of(row * 8, 8), 8)
+
+    def settle(at, *terms):
+        result = terms[0][...].astype(f32)
+        for each in terms[1:]:
+            result = result + each[...].astype(f32)
+        out_ref[at] = result.astype(bf16)
+
+    energy(0)
+    energy(1)
+    forward_y(1)
+    energy(2)
+    energy(3)
+    forward_y(0)
+    energy(4)
     landed(cross_x.at[2], cross_sem.at[2])
     add(first(2, 0), cross_x.at[2])
     copies.send(first(2, 0, 0, h_early), far_x.at[0], far_sem.at[2, 0], up)
@@ -593,13 +648,8 @@
     landed(cross_x.at[3], cross_sem.at[3])
     add(first(3, 0), cross_x.at[3])
     copies.send(first(3, 0, 0, h_early), near_x.at[1, pl.ds(0, h_early)], near_sem.at[2, 1, 0], down)
-
-    def both_near(j, ref):
-        count = ref.shape[1] // 2
-        for side in range(2):
-            for turn in range(2):
-                start = count if (side == 0) == (turn == 0) else 0
-                landed(ref.at[side, pl.ds(start, count)], near_sem.at[j, side, turn])
+    energy(5)
+    energy(6)
 
     both_near(1, near_y.at[1])
     add(late(0, 1), near_y.at[1, 0], near_y.at[1, 1])
@@ -612,42 +662,7 @@
     add(first(3, 0, h_early, h_early), far_x.at[1])
     copies.send(first(3, 0, h_early, h_early), near_x.at[1, pl.ds(h_early, h_early)], near_sem.at[2, 1, 1], down)
 
-    def settle(at, *terms):
-        result = terms[0][...].astype(f32)
-        for each in terms[1:]:
-            result = result + each[...].astype(f32)
-        result = result.astype(bf16)
-        out_ref[at] = result
-        for h in range(2):
-            total[h, at] = result[:, h * 128 : (h + 1) * 128].astype(f32)
-
-    def column(ref, l, start, count):
-        halves = [ref[h, pl.ds(start * 32 + l, count, stride=32), :].astype(bf16) for h in range(2)]
-        return jnp.concatenate(halves, 1)
-
-    def energy(start):
-        result = jnp.zeros((TILE // 2, TILE), f32)
-        for l in range(32):
-            result = result + lax.dot_general(
-                column(total, l, start, TILE // 2),
-                column(other, l, 0, TILE),
-                (((1,), (1,)), ((), ())),
-                preferred_element_type=f32,
-            )
-        tile[start : start + TILE // 2] = jnp.concatenate([-result, jnp.zeros_like(result)], 1)
-
-    both_near(0, near_y.at[0])
-    landed(cross_x.at[0], cross_sem.at[0])
-    landed(cross_y, cross_sem.at[4])
-    settle(pl.ds(0, LATE), late(0, 0), near_y.at[0, 0], near_y.at[0, 1], cross_y)
-    energy(0)
-    both_near(2, near_x)
-    settle(pl.ds(LATE, early), first(0, 0), cross_x.at[0], near_x.at[0], near_x.at[1])
-    energy(TILE // 2)
-
-    def share_of(row):
-        return pl.ds(pl.multiple_of(row * 8, 8), 8)
-
+    energy(7)
     for s in range(1, 8):
         target = in_row(s // 2, s % 2)
         copies.send(tile.at[share_of(target[0])], tile_row.at[s], row_sem.at[s], target)
@@ -658,20 +673,27 @@
     row_sum[...] = mine
     for d in range(1, 16):
         copies.send(row_sum, tile_col.at[d], col_sem.at[d], in_col(d))
+
+    both_near(0, near_y.at[0])
+    landed(cross_x.at[0], cross_sem.at[0])
+    landed(cross_y, cross_sem.at[4])
+    settle(pl.ds(0, LATE), late(0, 0), near_y.at[0, 0], near_y.at[0, 1], cross_y)
     for d in range(1, 16):
         landed(tile_col.at[d], col_sem.at[d])
         mine = mine + tile_col[d]
-    turned = pltpu.roll(mine, lax.rem(128 - 4 * col, 128), 1).T
+    turned = pltpu.roll(-mine, lax.rem(128 - 4 * col, 128), 1).T
     energy_ref[...] = turned[:4]
+    both_near(2, near_x)
+    settle(pl.ds(LATE, early), first(0, 0), cross_x.at[0], near_x.at[0], near_x.at[1])
     copies.finish()
 
 
-SCREEN_SCRATCH = 27
+SCREEN_SCRATCH = 26
 
 
 def kernel(*refs):
-    inputs, (screened, contracted, energy, panel_t), scratch = refs[:7], refs[7:11], refs[11:]
-    dressed, (first, second) = scratch[0], (scratch[1 : 1 + SCREEN_SCRATCH], scratch[1 + SCREEN_SCRATCH :])
+    inputs, (screened, contracted, energy, panel_t, dressed), scratch = refs[:7], refs[7:12], refs[12:]
+    first, second = scratch[:SCREEN_SCRATCH], scratch[SCREEN_SCRATCH:]
     flat = first[9]
     steps = contract_part(screened, panel_t, dressed, contracted, energy, *second[:8], flat, *second[8:])
     finish = screen_part(*inputs, screened, panel_t, dressed, lambda: next(steps), *first)
@@ -699,12 +721,11 @@
         pltpu.VMEM((2, 128, 16, NL), bf16),
         pltpu.VMEM((2, 128 * 16, 128), f32),
         pltpu.VMEM((2, 8, 16 * 32, 128), bf16),
-        pltpu.VMEM((2, 16 * 32, 128), bf16),
         pltpu.VMEM(panel_mask.shape, jnp.int32),
         pltpu.VMEM(near_mask.shape, jnp.int32),
         pltpu.VMEM((rows, NL), f32),
         pltpu.VMEM((cols, NL), f32),
-        pltpu.VMEM((32, NL), bf16),
+        pltpu.VMEM((NL, NL), bf16),
         dma((96,)),
         dma,
         dma((3,)),
@@ -726,12 +747,13 @@
         pltpu.VMEM((2, early // 2, cols), bf16),
         pltpu.VMEM((2, early, cols), bf16),
         pltpu.VMEM((2, long, 128), f32),
+        pltpu.VMEM((long, cols), bf16),
         pltpu.VMEM((TILE, 128), f32),
         pltpu.VMEM((8, 128), f32),
         pltpu.VMEM((8, 8, 128), f32),
         pltpu.VMEM((16, 8, 128), f32),
         dma((48,)),
-        dma((2,)),
+        dma((3,)),
         dma((3, 2)),
         dma((3, 2, 2)),
         dma((5,)),
@@ -746,10 +768,11 @@
             jax.ShapeDtypeStruct((long, cols), bf16),
             jax.ShapeDtypeStruct((4, 8), f32),
             jax.ShapeDtypeStruct((8, long, rows), bf16),
+            jax.ShapeDtypeStruct((8, long, cols), bf16),
         ),
         in_specs=[hbm] * 7,
-        out_specs=(vmem, vmem, vmem, hbm),
-        scratch_shapes=[pltpu.VMEM((long, cols), bf16)] + first + second,
+        out_specs=(vmem, vmem, vmem, hbm, hbm),
+        scratch_shapes=first + second,
         compiler_params=pltpu.CompilerParams(
             collective_id=0, has_side_effects=True, vmem_limit_bytes=64 * 2**20 - 2**16
         ),
@@ -758,11 +781,20 @@
 
 
 def hand_over_kernel(*refs):
-    sources, results, sem = refs[:3], refs[3:6], refs[6]
-    copies = [pltpu.make_async_copy(sources[i], results[i], sem.at[i]) for i in range(3)]
-    for copy in copies:
+    sources, results, held, sem = refs[:3], refs[3:6], refs[6:9], refs[9]
+    pieces = []
+    for k, source in enumerate(sources):
+        count = 4 if k == 1 else 1
+        size = source.shape[0] // count
+        pieces += [(k, pl.ds(i * size, size)) for i in range(count)]
+    taken = [pltpu.make_async_copy(sources[k].at[at], held[k].at[at], sem.at[0, i]) for i, (k, at) in enumerate(pieces)]
+    given = [pltpu.make_async_copy(held[k].at[at], results[k].at[at], sem.at[1, i]) for i, (k, at) in enumerate(pieces)]
+    for copy in taken:
         copy.start()
-    for copy in copies:
+    for i, copy in enumerate(given):
+        taken[i].wait()
+        copy.start()
+    for copy in given:
         copy.wait()
 
 
@@ -773,7 +805,8 @@
         out_shape=tuple(jax.ShapeDtypeStruct(array.shape, array.dtype) for array in arrays),
         in_specs=[hbm] * 3,
         out_specs=(hbm,) * 3,
-        scratch_shapes=[pltpu.SemaphoreType.DMA((3,))],
+        scratch_shapes=[pltpu.VMEM(array.shape, array.dtype) for array in arrays]
+        + [pltpu.SemaphoreType.DMA((2, 6))],
         name="hand_over",
     )(*arrays)
 
@@ -782,7 +815,7 @@
     polarization, metric, three_panel, three_near, green_function, mask_panel, mask_near
 ):
     near_cols = metric.shape[1]
-    screened, contracted, energy, _ = tile_terms(
+    screened, contracted, energy, *_ = tile_terms(
         polarization, metric, three_panel, three_near, mask_panel.T, mask_near.T, green_function
     )
     screened, contracted, energy = hand_over(screened, contracted, energy)

time: 218 us -> 174 us (0.80)
  Pallas kernels: 216 us -> 172 us
    pallas_call x1, Pallas kernels: 40.9 us -> 2.1 us  [hand_over(): pl.pallas_call(hand_over_kernel, out_shape=tuple((jax.ShapeDtypeStruct(ar...]
    pallas_call x1, Pallas kernels: 175 us -> 170 us  [tile_terms(): pl.pallas_call(kernel, out_shape=(jax.ShapeDtypeStruct((rows, cols), bf16...]
where the time goes in v6:
time: 174 us; the launch traced here: 173 us
  Pallas kernels  172 us (99%)
    pallas_call x1, Pallas kernels, tile_terms(): pl.pallas_call(kernel, out_shape=(jax.ShapeDtypeStruct((rows, cols), bf16...  170 us

profile of v6, /device:TPU:1, one launch (start us, length us, event | category | flops | bytes accessed | tf_op | source)
XLA Modules:
  0.0 172.9 jit_solution(5886078660349497772)
XLA Ops:
  0.6 170.0 %tile_terms.1 = (bf16[512,256]{1,0:T(8,128)(2,1)}, bf16[2048,256]{1,0:T(8,128)(2,1)}, f32[4,8]{1,0:T(4,128)}, bf16[8,2048,512]{2,1,0:T(8,128)(2,1)}, bf16[8,2048,256]{2,1,0:T(8,128)(2,1)}) custom-call(bf16[512,1664]{1,0:T(8,128)(2,1)} %refs_0_.1, bf16[3328,256]{1,0:T(8,128)(2,1)} %refs_1_.1, bf16[512,64,256]{2,1,0:T(8,128)(2,1)} %refs_2_.1, ...), custom_call_target="tpu_custom_call" | custom-call | tf_op jit(solution)/shard_map/tile_terms/pallas_call | solution.py:764
  170.6 2.1 %hand_over.1 = (bf16[512,256]{1,0:T(8,128)(2,1)}, bf16[2048,256]{1,0:T(8,128)(2,1)}, f32[4,8]{1,0:T(4,128)}) custom-call(bf16[512,256]{1,0:T(8,128)(2,1)} %get-tuple-element.9.refs_0_, bf16[2048,256]{1,0:T(8,128)(2,1)} %get-tuple-element.10.refs_1_, f32[4,8]{1,0:T(4,128)} %get-tuple-element.11.refs_2_), custom_call_target="tpu_custom_call" | custom-call | tf_op jit(solution)/shard_map/hand_over/pallas_call | solution.py:803

commit v7 on v6

--- a/solution.py
+++ b/solution.py
@@ -370,31 +370,29 @@
     total[...] = jnp.zeros_like(total)
     finish_masks()
 
-    panel_steps(0, 4)
+    panel_steps(0, 6)
+    for p in range(2):
+        a_outer_along_x(p)
     go_on(B, 0, 0)
     go_on(A, 0, 0)
-    panel_steps(4, 8)
+    panel_steps(6, 12)
     go_on(B, 0, 1)
     go_on(A, 0, 1)
     arrive(1, 0)
-    for p in range(2):
-        a_outer_along_x(p)
-    panel_steps(8, 11)
+    panel_steps(12, 16)
+    near_steps(0, 4)
     for p in range(2):
         far(B, 0, p)
         far(A, 0, p)
     arrive(1, 1)
     for p in range(2):
         b_outer_along_x(p)
-    panel_steps(11, 14)
     go_on(A, 1, 0)
     go_on(B, 1, 0)
-    panel_steps(14, 16)
-    near_steps(0, 2)
-    arrive(2, 0)
+    near_steps(4, 8)
     go_on(A, 1, 1)
     go_on(B, 1, 1)
-    near_steps(2, 4)
+    arrive(2, 0)
     for p in range(2):
         from_twin(0, p, (1, 2, 3))
     b_local.wait()
@@ -409,10 +407,9 @@
 
     far(A, 1, 0)
     far(B, 1, 0)
-    arrive(2, 1)
-    near_steps(4, 8)
     from_twin(1, 0, (0, 1, 2, 3))
     others(0)
+    arrive(2, 1)
     far(A, 1, 1)
     far(B, 1, 1)
     go_on(A, 2, 0)
@@ -675,16 +672,23 @@
         copies.send(row_sum, tile_col.at[d], col_sem.at[d], in_col(d))
 
     both_near(0, near_y.at[0])
-    landed(cross_x.at[0], cross_sem.at[0])
-    landed(cross_y, cross_sem.at[4])
-    settle(pl.ds(0, LATE), late(0, 0), near_y.at[0, 0], near_y.at[0, 1], cross_y)
+    for h in range(2):
+        lanes = slice(h * 128, (h + 1) * 128)
+        total[h, :LATE] = (
+            part[0, :LATE, lanes].astype(f32) + near_y[0, 0, :, lanes].astype(f32) + near_y[0, 1, :, lanes].astype(f32)
+        )
     for d in range(1, 16):
         landed(tile_col.at[d], col_sem.at[d])
         mine = mine + tile_col[d]
     turned = pltpu.roll(-mine, lax.rem(128 - 4 * col, 128), 1).T
     energy_ref[...] = turned[:4]
+    landed(cross_x.at[0], cross_sem.at[0])
     both_near(2, near_x)
     settle(pl.ds(LATE, early), first(0, 0), cross_x.at[0], near_x.at[0], near_x.at[1])
+    landed(cross_y, cross_sem.at[4])
+    for h in range(2):
+        lanes = slice(h * 128, (h + 1) * 128)
+        out_ref[:LATE, lanes] = (total[h, :LATE] + cross_y[:, lanes].astype(f32)).astype(bf16)
     copies.finish()
 
 

time: 174 us -> 170 us (0.977)
  Pallas kernels: 172 us -> 168 us
    pallas_call x1, Pallas kernels: 170 us -> 166 us  [tile_terms(): pl.pallas_call(kernel, out_shape=(jax.ShapeDtypeStruct((rows, cols), bf16...]
where the time goes in v7:
time: 170 us; the launch traced here: 169 us
  Pallas kernels  168 us (99%)
    pallas_call x1, Pallas kernels, tile_terms(): pl.pallas_call(kernel, out_shape=(jax.ShapeDtypeStruct((rows, cols), bf16...  166 us

profile of v7, /device:TPU:1, one launch (start us, length us, event | category | flops | bytes accessed | tf_op | source)
XLA Modules:
  0.0 168.8 jit_solution(15779560612530746407)
XLA Ops:
  0.6 165.9 %tile_terms.1 = (bf16[512,256]{1,0:T(8,128)(2,1)}, bf16[2048,256]{1,0:T(8,128)(2,1)}, f32[4,8]{1,0:T(4,128)}, bf16[8,2048,512]{2,1,0:T(8,128)(2,1)}, bf16[8,2048,256]{2,1,0:T(8,128)(2,1)}) custom-call(bf16[512,1664]{1,0:T(8,128)(2,1)} %refs_0_.1, bf16[3328,256]{1,0:T(8,128)(2,1)} %refs_1_.1, bf16[512,64,256]{2,1,0:T(8,128)(2,1)} %refs_2_.1, ...), custom_call_target="tpu_custom_call" | custom-call | tf_op jit(solution)/shard_map/tile_terms/pallas_call | solution.py:768
  166.5 2.1 %hand_over.1 = (bf16[512,256]{1,0:T(8,128)(2,1)}, bf16[2048,256]{1,0:T(8,128)(2,1)}, f32[4,8]{1,0:T(4,128)}) custom-call(bf16[512,256]{1,0:T(8,128)(2,1)} %get-tuple-element.9.refs_0_, bf16[2048,256]{1,0:T(8,128)(2,1)} %get-tuple-element.10.refs_1_, f32[4,8]{1,0:T(4,128)} %get-tuple-element.11.refs_2_), custom_call_target="tpu_custom_call" | custom-call | tf_op jit(solution)/shard_map/hand_over/pallas_call | solution.py:807

commit v8 on v7

--- a/solution.py
+++ b/solution.py
@@ -208,7 +208,8 @@
 
     barrier = pltpu.get_barrier_semaphore()
     partners = [device(lax.rem(y + k // 2, 4), lax.rem(xh + k, 2), z, xl, core) for k in range(1, 8)]
-    partners += [(row, lax.rem(col + k, 16)) for k in range(1, 16)]
+    partners += [device(y, xh, lax.rem(z + k, 4), xl, core) for k in range(1, 4)]
+    partners += [twin, device(y, xh, z, 1 - xl, core), device(y, xh, z, 1 - xl, 1 - core)]
     partners.append(device(y, 1 - xh, z, 1 - xl, core))
     for partner in partners:
         pl.semaphore_signal(barrier, inc=1, device_id=partner, device_id_type=MESH)
@@ -429,27 +430,25 @@
 
         return step
 
-    step = own(0)
     for d in (0, 1, 3):
-        step(d)
+        own(0)(d)
     go_on(A, 2, 1)
     go_on(B, 2, 1)
-    far(A, 2, 0)
-    far(B, 2, 0)
-    from_twin(2, 0, (2,))
     from_twin(2, 1, (0, 1, 3))
-    step(2)
-    step = own(1)
     for d in (0, 1, 3):
-        step(d)
+        own(1)(d)
     ahead()
-    far(B, 2, 1)
-    keep_rows(y_at[2], 1, 1)
-    far(A, 2, 1)
     landed(take.at[0], last_sem.at[0])
     landed(take.at[1], last_sem.at[1])
-    total[0, 1] += total[1, 1] + take[0].astype(jnp.float32) + take[1].astype(jnp.float32)
-    total[1, 1] = jnp.zeros_like(total[1, 1])
+    total[0, 1] += take[0].astype(jnp.float32) + take[1].astype(jnp.float32)
+    far(B, 2, 0)
+    far(A, 2, 0)
+    keep_rows(y_at[2], 0, 1)
+    from_twin(2, 0, (2,))
+    keep_cols(z_at[2], 0, 1)
+    far(B, 2, 1)
+    far(A, 2, 1)
+    keep_rows(y_at[2], 1, 1)
     from_twin(2, 1, (2,))
     keep_cols(z_at[2], 1, 1)
     out_ref[...] = (total[0, 1] + total[1, 1]).astype(jnp.bfloat16)
@@ -507,9 +506,6 @@
     def in_row(d, j):
         return device(lax.rem(y + d, 4), lax.rem(xh + j, 2), z, xl, core)
 
-    def in_col(d):
-        return (y * 2 + xh, lax.rem(col + d, 16))
-
     order = [(2, 1), (2, 0), (1, 1), (3, 1), (1, 0), (3, 0), (0, 1), (0, 0)]
     chunk = block.shape[1]
 
@@ -647,6 +643,10 @@
     copies.send(first(3, 0, 0, h_early), near_x.at[1, pl.ds(0, h_early)], near_sem.at[2, 1, 0], down)
     energy(5)
     energy(6)
+    energy(7)
+    for s in range(1, 8):
+        target = in_row(s // 2, s % 2)
+        copies.send(tile.at[share_of(target[0])], tile_row.at[s], row_sem.at[s], target)
 
     both_near(1, near_y.at[1])
     add(late(0, 1), near_y.at[1, 0], near_y.at[1, 1])
@@ -659,17 +659,19 @@
     add(first(3, 0, h_early, h_early), far_x.at[1])
     copies.send(first(3, 0, h_early, h_early), near_x.at[1, pl.ds(h_early, h_early)], near_sem.at[2, 1, 1], down)
 
-    energy(7)
-    for s in range(1, 8):
-        target = in_row(s // 2, s % 2)
-        copies.send(tile.at[share_of(target[0])], tile_row.at[s], row_sem.at[s], target)
     mine = tile[share_of(y * 2 + xh)]
     for s in range(1, 8):
         landed(tile_row.at[s], row_sem.at[s])
         mine = mine + tile_row[s]
-    row_sum[...] = mine
-    for d in range(1, 16):
-        copies.send(row_sum, tile_col.at[d], col_sem.at[d], in_col(d))
+    along_z = [device(y, xh, lax.rem(z + d, 4), xl, core) for d in range(1, 4)]
+    close = [device(y, xh, z, xl, 1 - core), device(y, xh, z, 1 - xl, core), device(y, xh, z, 1 - xl, 1 - core)]
+    for turn, targets in enumerate((along_z, close)):
+        row_sum[turn] = mine
+        for d, target in enumerate(targets):
+            copies.send(row_sum.at[turn], tile_col.at[turn * 3 + d], col_sem.at[turn * 3 + d], target)
+        for d in range(turn * 3, turn * 3 + 3):
+            landed(tile_col.at[d], col_sem.at[d])
+            mine = mine + tile_col[d]
 
     both_near(0, near_y.at[0])
     for h in range(2):
@@ -677,9 +679,6 @@
         total[h, :LATE] = (
             part[0, :LATE, lanes].astype(f32) + near_y[0, 0, :, lanes].astype(f32) + near_y[0, 1, :, lanes].astype(f32)
         )
-    for d in range(1, 16):
-        landed(tile_col.at[d], col_sem.at[d])
-        mine = mine + tile_col[d]
     turned = pltpu.roll(-mine, lax.rem(128 - 4 * col, 128), 1).T
     energy_ref[...] = turned[:4]
     landed(cross_x.at[0], cross_sem.at[0])
@@ -753,16 +752,16 @@
         pltpu.VMEM((2, long, 128), f32),
         pltpu.VMEM((long, cols), bf16),
         pltpu.VMEM((TILE, 128), f32),
-        pltpu.VMEM((8, 128), f32),
+        pltpu.VMEM((2, 8, 128), f32),
         pltpu.VMEM((8, 8, 128), f32),
-        pltpu.VMEM((16, 8, 128), f32),
+        pltpu.VMEM((6, 8, 128), f32),
         dma((48,)),
         dma((3,)),
         dma((3, 2)),
         dma((3, 2, 2)),
         dma((5,)),
         dma((8,)),
-        dma((16,)),
+        dma((6,)),
     ]
     assert len(first) == SCREEN_SCRATCH
     return pl.pallas_call(

time: 170 us -> 167 us (0.982)
  Pallas kernels: 168 us -> 165 us
    pallas_call x1, Pallas kernels: 166 us -> 163 us  [tile_terms(): pl.pallas_call(kernel, out_shape=(jax.ShapeDtypeStruct((rows, cols), bf16...]
where the time goes in v8:
time: 167 us; the launch traced here: 166 us
  Pallas kernels  165 us (99%)
    pallas_call x1, Pallas kernels, tile_terms(): pl.pallas_call(kernel, out_shape=(jax.ShapeDtypeStruct((rows, cols), bf16...  163 us

profile of v8, /device:TPU:1, one launch (start us, length us, event | category | flops | bytes accessed | tf_op | source)
XLA Modules:
  0.0 165.7 jit_solution(16737644716352049668)
XLA Ops:
  0.6 162.7 %tile_terms.1 = (bf16[512,256]{1,0:T(8,128)(2,1)}, bf16[2048,256]{1,0:T(8,128)(2,1)}, f32[4,8]{1,0:T(4,128)}, bf16[8,2048,512]{2,1,0:T(8,128)(2,1)}, bf16[8,2048,256]{2,1,0:T(8,128)(2,1)}) custom-call(bf16[512,1664]{1,0:T(8,128)(2,1)} %refs_0_.1, bf16[3328,256]{1,0:T(8,128)(2,1)} %refs_1_.1, bf16[512,64,256]{2,1,0:T(8,128)(2,1)} %refs_2_.1, ...), custom_call_target="tpu_custom_call" | custom-call | tf_op jit(solution)/shard_map/tile_terms/pallas_call | solution.py:767
  163.4 2.1 %hand_over.1 = (bf16[512,256]{1,0:T(8,128)(2,1)}, bf16[2048,256]{1,0:T(8,128)(2,1)}, f32[4,8]{1,0:T(4,128)}) custom-call(bf16[512,256]{1,0:T(8,128)(2,1)} %get-tuple-element.9.refs_0_, bf16[2048,256]{1,0:T(8,128)(2,1)} %get-tuple-element.10.refs_1_, f32[4,8]{1,0:T(4,128)} %get-tuple-element.11.refs_2_), custom_call_target="tpu_custom_call" | custom-call | tf_op jit(solution)/shard_map/hand_over/pallas_call | solution.py:806

commit v9 on v8

--- a/solution.py
+++ b/solution.py
@@ -25,10 +25,10 @@
 
 class Copies:
     def __init__(self, send_sem):
-        self.send_sem, self.started = send_sem, []
+        self.send_sem, self.started, self.count = send_sem, [], 0
 
     def send(self, src, dst, recv_sem, target):
-        index = len(self.started)
+        index, self.count = self.count, self.count + 1
         copy = pltpu.make_async_remote_copy(
             src_ref=src,
             dst_ref=dst,
@@ -41,7 +41,7 @@
         self.started.append((copy, None))
 
     def send_if(self, wanted, src, dst, recv_sem, target):
-        index = len(self.started)
+        index, self.count = self.count, self.count + 1
         copy = pltpu.make_async_remote_copy(
             src_ref=src,
             dst_ref=dst,
@@ -53,12 +53,14 @@
         pl.when(wanted)(copy.start)
         self.started.append((copy, wanted))
 
-    def finish(self):
-        for copy, wanted in self.started:
+    def finish(self, but=0):
+        done = len(self.started) - but
+        for copy, wanted in self.started[:done]:
             if wanted is None:
                 copy.wait_send()
             else:
                 pl.when(wanted)(copy.wait_send)
+        self.started = self.started[done:]
 
 
 def landed(ref, sem):
@@ -381,7 +383,7 @@
     go_on(A, 0, 1)
     arrive(1, 0)
     panel_steps(12, 16)
-    near_steps(0, 4)
+    near_steps(0, 3)
     for p in range(2):
         far(B, 0, p)
         far(A, 0, p)
@@ -390,7 +392,7 @@
         b_outer_along_x(p)
     go_on(A, 1, 0)
     go_on(B, 1, 0)
-    near_steps(4, 8)
+    near_steps(3, 8)
     go_on(A, 1, 1)
     go_on(B, 1, 1)
     arrive(2, 0)
@@ -635,19 +637,18 @@
     add(first(2, 0), cross_x.at[2])
     copies.send(first(2, 0, 0, h_early), far_x.at[0], far_sem.at[2, 0], up)
     copies.send(first(2, 0, h_early, h_early), far_x.at[1], far_sem.at[2, 1], down)
+    energy(5)
     landed(cross_x.at[1], cross_sem.at[1])
     add(first(1, 0), cross_x.at[1])
     copies.send(first(1, 0, h_early, h_early), near_x.at[0, pl.ds(h_early, h_early)], near_sem.at[2, 0, 0], up)
-    landed(cross_x.at[3], cross_sem.at[3])
-    add(first(3, 0), cross_x.at[3])
-    copies.send(first(3, 0, 0, h_early), near_x.at[1, pl.ds(0, h_early)], near_sem.at[2, 1, 0], down)
-    energy(5)
     energy(6)
     energy(7)
     for s in range(1, 8):
         target = in_row(s // 2, s % 2)
         copies.send(tile.at[share_of(target[0])], tile_row.at[s], row_sem.at[s], target)
-
+    landed(cross_x.at[3], cross_sem.at[3])
+    add(first(3, 0), cross_x.at[3])
+    copies.send(first(3, 0, 0, h_early), near_x.at[1, pl.ds(0, h_early)], near_sem.at[2, 1, 0], down)
     both_near(1, near_y.at[1])
     add(late(0, 1), near_y.at[1, 0], near_y.at[1, 1])
     copies.send(late(0, 1), cross_y, cross_sem.at[4], across)
@@ -673,6 +674,9 @@
             landed(tile_col.at[d], col_sem.at[d])
             mine = mine + tile_col[d]
 
+    copies.finish(but=9)
+    yield
+
     both_near(0, near_y.at[0])
     for h in range(2):
         lanes = slice(h * 128, (h + 1) * 128)
@@ -684,6 +688,8 @@
     landed(cross_x.at[0], cross_sem.at[0])
     both_near(2, near_x)
     settle(pl.ds(LATE, early), first(0, 0), cross_x.at[0], near_x.at[0], near_x.at[1])
+    yield
+
     landed(cross_y, cross_sem.at[4])
     for h in range(2):
         lanes = slice(h * 128, (h + 1) * 128)
@@ -695,13 +701,26 @@
 
 
 def kernel(*refs):
-    inputs, (screened, contracted, energy, panel_t, dressed), scratch = refs[:7], refs[7:12], refs[12:]
+    inputs, (screened_out, contracted_out, energy, panel_t, dressed), scratch = refs[:7], refs[7:12], refs[12:]
+    (screened, contracted, out_sem), scratch = scratch[:3], scratch[3:]
     first, second = scratch[:SCREEN_SCRATCH], scratch[SCREEN_SCRATCH:]
     flat = first[9]
+    leaving = [
+        pltpu.make_async_copy(screened, screened_out, out_sem.at[0]),
+        pltpu.make_async_copy(contracted.at[pl.ds(LATE, TILE * 32 - LATE)], contracted_out.at[pl.ds(LATE, TILE * 32 - LATE)], out_sem.at[1]),
+        pltpu.make_async_copy(contracted.at[pl.ds(0, LATE)], contracted_out.at[pl.ds(0, LATE)], out_sem.at[2]),
+    ]
     steps = contract_part(screened, panel_t, dressed, contracted, energy, *second[:8], flat, *second[8:])
     finish = screen_part(*inputs, screened, panel_t, dressed, lambda: next(steps), *first)
+    leaving[0].start()
+    next(steps)
+    finish()
+    next(steps)
+    leaving[1].start()
     next(steps, None)
-    finish()
+    leaving[2].start()
+    for copy in leaving:
+        copy.wait()
 
 
 def tile_terms(a, b, panel, near, panel_mask, near_mask, green):
@@ -774,8 +793,8 @@
             jax.ShapeDtypeStruct((8, long, cols), bf16),
         ),
         in_specs=[hbm] * 7,
-        out_specs=(vmem, vmem, vmem, hbm, hbm),
-        scratch_shapes=first + second,
+        out_specs=(hbm, hbm, vmem, hbm, hbm),
+        scratch_shapes=[pltpu.VMEM((rows, cols), bf16), pltpu.VMEM((long, cols), bf16), dma((3,))] + first + second,
         compiler_params=pltpu.CompilerParams(
             collective_id=0, has_side_effects=True, vmem_limit_bytes=64 * 2**20 - 2**16
         ),

time: 167 us -> 166 us (level)
  no operation moved by 1% of the time
where the time goes in v9:
time: 166 us; the launch traced here: 165 us
  Pallas kernels  164 us (99%)
    pallas_call x1, Pallas kernels, tile_terms(): pl.pallas_call(kernel, out_shape=(jax.ShapeDtypeStruct((rows, cols), bf16...  162 us

profile of v9, /device:TPU:1, one launch (start us, length us, event | category | flops | bytes accessed | tf_op | source)
XLA Modules:
  0.0 165.1 jit_solution(13649550190273146539)
XLA Ops:
  0.6 162.2 %tile_terms.1 = (bf16[512,256]{1,0:T(8,128)(2,1)}, bf16[2048,256]{1,0:T(8,128)(2,1)}, f32[4,8]{1,0:T(4,128)}, bf16[8,2048,512]{2,1,0:T(8,128)(2,1)}, bf16[8,2048,256]{2,1,0:T(8,128)(2,1)}) custom-call(bf16[512,1664]{1,0:T(8,128)(2,1)} %refs_0_.1, bf16[3328,256]{1,0:T(8,128)(2,1)} %refs_1_.1, bf16[512,64,256]{2,1,0:T(8,128)(2,1)} %refs_2_.1, ...), custom_call_target="tpu_custom_call" | custom-call | tf_op jit(solution)/shard_map/tile_terms/pallas_call | solution.py:786
  162.8 2.1 %hand_over.1 = (bf16[512,256]{1,0:T(8,128)(2,1)}, bf16[2048,256]{1,0:T(8,128)(2,1)}, f32[4,8]{1,0:T(4,128)}) custom-call(bf16[512,256]{1,0:T(8,128)(2,1)} %get-tuple-element.9.refs_0_, bf16[2048,256]{1,0:T(8,128)(2,1)} %get-tuple-element.10.refs_1_, f32[4,8]{1,0:T(4,128)} %get-tuple-element.11.refs_2_), custom_call_target="tpu_custom_call" | custom-call | tf_op jit(solution)/shard_map/hand_over/pallas_call | solution.py:825
